TPU v7x, 512 devices: a whole 4x4x16 slice. The times are simulated.
512 devices in a mesh: ctx: 64 (over z, x_hi, core), head: 8 (over y, x_lo).
Axes of the slice: x: 4 (x_hi: 2, x_lo: 2; x = x_hi * 2 + x_lo), y: 4, z: 16, core: 2. Of those that a mesh axis runs over, the one named last changes fastest.
Arguments:
- queries: bfloat16 [8192, 8192], P('ctx', 'head'), may hold values from -6 to 6
- q_gain: float32 [128], replicated, may hold values from 0.5 to 2.5
- k_gain: float32 [128], replicated, may hold values from 0.5 to 2.5
- attn_gate: float32 [1], replicated, may hold values from 0.3 to 1.5
- vision: bfloat16 [8192, 8192], P('ctx', 'head'), may hold values from -6 to 6
- key_projection_matrix: bfloat16 [8192, 1024], P('ctx', 'head'), may hold values from -0.0625 to 0.0625
- value_projection_matrix: bfloat16 [8192, 1024], P('ctx', 'head'), may hold values from -0.0625 to 0.0625
- image_start: int32 [24], replicated, may hold values from 1 to 8191, as said below
- slot_image: int32 [128], replicated, may hold values from 0 to 24, as said below
Outputs:
- attended: bfloat16 [8192, 8192], P('ctx', 'head')
Inputs may be any that keep to these rules, and one draw needn't show every extreme that they name: `image_start`: strictly increasing; the first image stands at position 1 and the last at 8191. `slot_image`: value 24 marks an empty slot. Each image has 3 to 4 tiles and some image exactly 4. Used slots are each device's lowest slots, and the numbers of used slots of two devices differ by at most one.
All inputs are finite; a program needn't handle non-finite values.
Results may differ from a plain program's by a relative error of at most 0.011.
Values may be sent and summed in bfloat16 or wider, within the bound.
No kernel may reach another device: no remote copies, remote signals or barrier semaphores. Data moves between devices by JAX's collectives and lax.ppermute only.
A program may use at most 64 MiB of HBM per device.

v0:
```python
import math

import jax
import jax.numpy as jnp
from jax import lax
from jax.sharding import PartitionSpec as P

EPS = 1e-05


def rms_scale(raw, gain):
    return raw * lax.rsqrt(jnp.mean(raw * raw, axis=-1, keepdims=True) + EPS) * gain


def add_rows(state, query_block, position, key_rows, value_rows, row_begin, scale):
    numer, denom = state
    count = query_block.shape[0]
    kv_heads = key_rows.shape[1]
    grouped_heads = query_block.reshape(count, kv_heads, -1, key_rows.shape[2])
    scores = (
        jnp.einsum("qkgd,tkd->qkgt", grouped_heads, key_rows, preferred_element_type=jnp.float32)
        * scale
    )
    visible = (row_begin[None, :] <= position[:, None])[:, None, None, :]
    weights = jnp.where(visible, jnp.exp(scores), 0.0)
    denom = denom + jnp.sum(weights, axis=-1).reshape(denom.shape)
    update = jnp.einsum(
        "qkgt,tkd->qkgd",
        weights.astype(jnp.bfloat16),
        value_rows,
        preferred_element_type=jnp.float32,
    )
    return (numer + update.reshape(numer.shape), denom)


def local(
    queries,
    q_gain,
    k_gain,
    attn_gate,
    vision,
    key_projection_matrix,
    value_projection_matrix,
    image_start,
    slot_image,
):
    ctx_size = lax.axis_size("ctx")
    own_index = lax.axis_index("ctx")
    head_dim = q_gain.shape[0]
    tok_rows = queries.shape[0]
    shard_rows = vision.shape[0]
    slots_here = slot_image.shape[0] // ctx_size
    tile_rows = shard_rows // slots_here
    kv_cols = key_projection_matrix.shape[1]
    kv_heads = kv_cols // head_dim
    q_heads = queries.shape[1] // head_dim
    n_images = image_start.shape[0]
    total_tokens = tok_rows * ctx_size
    features = lax.all_gather(vision, "head", axis=1, tiled=True)
    unnormed_keys = jnp.dot(
        features,
        lax.all_gather(key_projection_matrix, "ctx", axis=0, tiled=True),
        preferred_element_type=jnp.float32,
    )
    values_raw = jnp.dot(
        features,
        lax.all_gather(value_projection_matrix, "ctx", axis=0, tiled=True),
        preferred_element_type=jnp.float32,
    )
    keys = (
        rms_scale(unnormed_keys.reshape(shard_rows, kv_heads, head_dim), k_gain)
        .astype(jnp.bfloat16)
        .reshape(shard_rows, kv_cols)
    )
    value_vectors = values_raw.astype(jnp.bfloat16)
    normalized_input = rms_scale(
        queries.astype(jnp.float32).reshape(tok_rows, q_heads, head_dim), q_gain
    ).astype(jnp.bfloat16)
    match = slot_image[:, None] == jnp.arange(n_images, dtype=jnp.int32)[None, :]
    slot_start = jnp.sum(jnp.where(match, image_start[None, :], 0), axis=1) + jnp.where(
        slot_image >= n_images, total_tokens, 0
    )
    slot_grid = slot_start.reshape(ctx_size, slots_here)
    own_positions = own_index * tok_rows + jnp.arange(tok_rows, dtype=jnp.int32)
    query_blocks = (normalized_input,)
    positions = (own_positions,)
    last_seen = tuple((jnp.max(position) for position in positions))
    scale = head_dim ** (-0.5)
    initial = tuple(
        (
            (
                jnp.zeros((query_block.shape[0], q_heads, head_dim), jnp.float32),
                jnp.zeros((query_block.shape[0], q_heads), jnp.float32),
            )
            for query_block in query_blocks
        )
    )
    key_piece = lax.all_gather(keys, "ctx", axis=0, tiled=True)
    value_piece = lax.all_gather(value_vectors, "ctx", axis=0, tiled=True)
    shard_total = key_piece.shape[0] // shard_rows
    units = math.gcd(shard_total, 8)
    unit_rows = units * tile_rows
    turns = shard_total // units * slots_here
    key_grid = key_piece.reshape(shard_total, slots_here, tile_rows, kv_cols)
    value_grid = value_piece.reshape(shard_total, slots_here, tile_rows, kv_cols)

    def one_unit(number, state):
        first = number // slots_here * units
        slot = number % slots_here
        zero = jnp.zeros((), jnp.int32)
        key_rows = lax.dynamic_slice(
            key_grid, (first, slot, zero, zero), (units, 1, tile_rows, kv_cols)
        ).reshape(unit_rows, kv_heads, head_dim)
        value_rows = lax.dynamic_slice(
            value_grid, (first, slot, zero, zero), (units, 1, tile_rows, kv_cols)
        ).reshape(unit_rows, kv_heads, head_dim)
        begins = lax.dynamic_slice(slot_grid, (first, slot), (units, 1)).reshape(units)
        row_begin = jnp.repeat(begins, tile_rows)
        earliest = jnp.min(begins)
        which = 0

        def compute(inner, which=which):
            return add_rows(
                inner, query_blocks[which], positions[which], key_rows, value_rows, row_begin, scale
            )

        def unchanged(inner):
            return inner

        updated = [lax.cond(earliest <= last_seen[which], compute, unchanged, state[which])]
        return tuple(updated)

    sums = lax.fori_loop(0, turns, one_unit, initial)
    factor = jnp.tanh(attn_gate[0])
    which = 0
    numer, denom = sums[which]
    seen_row = positions[which] >= image_start[0]
    safe = jnp.where(seen_row[:, None], denom, 1.0)[:, :, None]
    mixed = jnp.where(seen_row[:, None, None], factor * numer / safe, 0.0).astype(jnp.bfloat16)
    outputs = mixed.reshape(mixed.shape[0], q_heads * head_dim)
    return outputs


def solution(mesh):
    in_specs = (
        P("ctx", "head"),
        P(),
        P(),
        P(),
        P("ctx", "head"),
        P("ctx", "head"),
        P("ctx", "head"),
        P(),
        P(),
    )
    out_specs = P("ctx", "head")
    return jax.shard_map(local, mesh=mesh, in_specs=in_specs, out_specs=out_specs, check_vma=False)
```

profile of v0, /device:TPU:1, one launch (start us, length us, event | category | flops | bytes accessed | tf_op | source)
XLA Modules:
  0.0 694.8 jit_solution(1647651460169468813)
XLA Ops:
  6.5 0.7 all-gather.6.cloned.1.call-update
  7.3 0.7 all-gather.8.cloned.1.call-update
  8.1 0.7 all-gather.12.cloned.1.call-update
  8.8 65.6 %all-gather.6.cloned.1.call-done = bf16[128,8192]{1,0:T(8,128)(2,1)} async-done(((bf16[128,1024]{1,0:T(8,128)(2,1)}), bf16[128,8192]{1,0:T(8,128)(2,1)}) %all-gather.6.cloned.1.call-update) | async-done | bytes 2097168 | tf_op jit(solution)/shard_map/all_gather | solution.py:59
  74.4 147.1 %all-gather.8.cloned.1.call-done = bf16[8192,128]{1,0:T(8,128)(2,1)} async-done(((bf16[128,128]{1,0:T(8,128)(2,1)}), bf16[8192,128]{1,0:T(8,128)(2,1)}) %all-gather.8.cloned.1.call-update) | async-done | bytes 2097168 | tf_op jit(solution)/shard_map/all_gather | solution.py:62
  221.4 3.2 multiply_reduce_fusion
  224.6 0.7 multiply_convert_fusion
  225.4 137.5 %all-gather.12.cloned.1.call-done = bf16[8192,128]{1,0:T(8,128)(2,1)} async-done(((bf16[128,128]{1,0:T(8,128)(2,1)}), bf16[8192,128]{1,0:T(8,128)(2,1)}) %all-gather.12.cloned.1.call-update) | async-done | bytes 2097168 | tf_op jit(solution)/shard_map/all_gather | solution.py:67
  362.9 2.9 convolution_convert_fusion
  365.8 0.7 fusion.16
  368.2 129.3 %all-gather.10.cloned.1.call-done = bf16[8192,128]{0,1:T(8,128)(2,1)} async-done(((bf16[128,128]{0,1:T(8,128)(2,1)}), bf16[8192,128]{0,1:T(8,128)(2,1)}) %all-gather.10.cloned.1.call-update) | async-done | bytes 2097168 | tf_op jit(solution)/shard_map/all_gather | solution.py:98
  497.5 3.2 copy.24
  500.7 1.5 copy.27
  502.3 136.3 %all-gather.14.cloned.1.call-done = bf16[8192,128]{1,0:T(8,128)(2,1)} async-done(((bf16[128,128]{1,0:T(8,128)(2,1)}), bf16[8192,128]{1,0:T(8,128)(2,1)}) %all-gather.14.cloned.1.call-update) | async-done | bytes 2097168 | tf_op jit(solution)/shard_map/all_gather | solution.py:99
  638.5 1.8 copy.29
  640.4 47.0 %while.18 = (s32[]{:T(128)}, f32[128,8,128]{2,0,1:T(8,128)S(1)}, f32[128,8]{0,1:T(8,128)S(1)}, s32[64,2]{0,1:T(2,128)S(1)}, s32[]{:T(128)}, /*index=5*/bf16[64,2...) while((s32[]{:T(128)}, f32[128,8,128]{2,0,1:T(8,128)S(1)}, ...), condition=%wide.region_9.10_spmd.clone, body=%wide.region_4.9_spmd.clone.sunk | while | flops 271777952 | bytes 6515286 | solution.py:133
  640.4 0.7 fusion.28
  642.3 2.6 conditional.3
  642.7 0.9 constant_dynamic-slice_fusion
  644.2 0.7 convolution_add_fusion
  645.0 0.7 fusion.28
  646.9 2.6 conditional.3
  647.2 0.9 constant_dynamic-slice_fusion
  648.7 0.7 convolution_add_fusion
  649.5 0.7 fusion.28
  651.4 2.6 conditional.3
  651.7 0.9 constant_dynamic-slice_fusion
  653.3 0.7 convolution_add_fusion
  654.1 0.7 fusion.28
  656.0 2.6 conditional.3
  656.3 0.9 constant_dynamic-slice_fusion
  657.8 0.7 convolution_add_fusion
  658.6 0.7 fusion.28
  660.6 0.7 fusion.28
  662.5 2.6 conditional.3
  662.8 0.9 constant_dynamic-slice_fusion
  664.3 0.7 convolution_add_fusion
  665.1 0.7 fusion.28
  667.1 0.7 fusion.28
  669.1 0.7 fusion.28
  671.0 0.7 fusion.28
  673.0 0.7 fusion.28
  676.9 0.7 fusion.28
  678.9 2.6 conditional.3
  679.2 0.9 constant_dynamic-slice_fusion
  680.7 0.7 convolution_add_fusion
  683.5 0.7 fusion.28
  687.4 0.9 copy_bitcast_fusion
  (98 shorter events, 8.5 us)
Async XLA Ops:
  6.5 67.8 %all-gather.6.cloned.1.call-start = ((), (), s32[]{:S(2)}) async-start(), calls=%async_computation | async-start | bytes 2359296 | tf_op jit(solution)/shard_map/all_gather | solution.py:59
  7.3 214.2 %all-gather.8.cloned.1.call-start = ((), (), s32[]{:S(2)}) async-start(), calls=%async_computation.1 | async-start | bytes 2129920 | tf_op jit(solution)/shard_map/all_gather | solution.py:62
  8.0 354.9 %all-gather.12.cloned.1.call-start = ((), (), s32[]{:S(2)}) async-start(), calls=%async_computation.3 | async-start | bytes 2129920 | tf_op jit(solution)/shard_map/all_gather | solution.py:67
  8.7 215.9 %copy-start.2 = (f32[128]{0:T(128)S(1)}, f32[128]{0:T(128)}, u32[]{:S(2)}) copy-start(f32[128]{0:T(128)} %param.15) | copy-start | bytes 1540
  8.8 488.8 %all-gather.10.cloned.1.call-start = ((), (), s32[]{:S(2)}) async-start(), calls=%async_computation.2 | async-start | bytes 2129920 | tf_op jit(solution)/shard_map/all_gather | solution.py:98
  74.4 288.6 %copy-start = (bf16[128,8192]{1,0:T(8,128)(2,1)S(1)}, bf16[128,8192]{1,0:T(8,128)(2,1)}, u32[]{:S(2)}) copy-start(bf16[128,8192]{1,0:T(8,128)(2,1)} %all-gather.6.cloned.1.call-done) | copy-start | bytes 6291460
  225.3 141.9 %copy-start.4 = (s32[128]{0:T(128)S(1)}, s32[128]{0:T(128)}, u32[]{:S(2)}) copy-start(s32[128]{0:T(128)} %param.21) | copy-start | bytes 1540
  225.3 141.9 %copy-start.5 = (s32[24]{0:T(128)S(1)}, s32[24]{0:T(128)}, u32[]{:S(2)}) copy-start(s32[24]{0:T(128)} %param.20) | copy-start | bytes 292
  225.4 142.2 %copy-start.1 = (bf16[128,1024]{1,0:T(8,128)(2,1)S(1)}, bf16[128,1024]{1,0:T(8,128)(2,1)}, u32[]{:S(2)}) copy-start(bf16[128,1024]{1,0:T(8,128)(2,1)} %param.13) | copy-start | bytes 786436
  225.4 142.5 %copy-start.3 = (f32[128]{0:T(128)S(1)}, f32[128]{0:T(128)}, u32[]{:S(2)}) copy-start(f32[128]{0:T(128)} %param.14) | copy-start | bytes 1540
  225.4 413.2 %all-gather.14.cloned.1.call-start = ((), (), s32[]{:S(2)}) async-start(), calls=%async_computation.4 | async-start | bytes 2129920 | tf_op jit(solution)/shard_map/all_gather | solution.py:99
Sparse Core Ops, SparseCore 0:
  9.4 64.8 all-gather.5
  77.6 143.7 all-gather.7
  224.7 138.1 all-gather.11
  365.8 131.6 all-gather.9
  500.6 137.8 all-gather.13
where the time goes:
time: 702 us; the launch traced here: 695 us
  waiting for transfers between devices  618 us (88%)
  loops' own time  20.9 us (3%)
  other arithmetic  14.4 us (2%)
  between operations  14 us (2%)
  matrix products  13.9 us (2%)
  local copies, waits for them, and re-layouts  13.7 us (2%)
    all_gather x1, waiting for transfers between devices, local(): lax.all_gather(key_projection_matrix, 'ctx', axis=0, tiled=True)  147 us
    all_gather x1, waiting for transfers between devices, local(): lax.all_gather(value_projection_matrix, 'ctx', axis=0, tiled=True)  137 us
    all_gather x1, waiting for transfers between devices, local(): value_piece = lax.all_gather(value_vectors, 'ctx', axis=0, tiled=True)  136 us
    all_gather x1, waiting for transfers between devices, local(): key_piece = lax.all_gather(keys, 'ctx', axis=0, tiled=True)  129 us
    all_gather x1, waiting for transfers between devices, local(): features = lax.all_gather(vision, 'head', axis=1, tiled=True)  65.6 us
    another operation x1, loops' own time, local(): sums = lax.fori_loop(0, turns, one_unit, initial)  20.4 us
  transfers between devices with their start and end apart: 5, of which 5 were waited for; matrix products, arithmetic and copies ran while one was open for 2% of the time, Pallas kernels for 0%

commit v1 on v0

v1 whole, which is shorter than its diff:
```python
import functools
import math

import jax
import jax.numpy as jnp
from jax import lax
from jax.experimental import pallas as pl
from jax.experimental.pallas import tpu as pltpu
from jax.sharding import PartitionSpec as P

EPS = 1e-05
PLANE = 4
VMEM_LIMIT = 48 * 1024 * 1024


def params(**more):
    return pltpu.CompilerParams(vmem_limit_bytes=VMEM_LIMIT, **more)


def vmem():
    return pl.BlockSpec(memory_space=pltpu.VMEM)


def smem():
    return pl.BlockSpec(memory_space=pltpu.SMEM)


def project_kernel(x_ref, w_ref, out_ref):
    members, pieces, rows, depth = x_ref.shape
    total = None
    for piece in range(pieces):
        part = jnp.dot(
            x_ref[:, piece].reshape(members * rows, depth),
            w_ref[piece],
            preferred_element_type=jnp.float32,
        )
        total = part if total is None else total + part
    out_ref[...] = total.reshape(out_ref.shape).astype(out_ref.dtype)


def finish_kernel(parts_ref, gain_ref, out_ref):
    raw = jnp.sum(parts_ref[...].astype(jnp.float32), axis=0)
    head_dim = gain_ref.shape[1]
    keys = raw[:, :head_dim]
    mean = jnp.mean(keys * keys, axis=-1, keepdims=True)
    keys = keys * lax.rsqrt(mean + EPS) * gain_ref[...]
    both = jnp.concatenate([keys, raw[:, head_dim:]], axis=1).astype(out_ref.dtype)
    for copy in range(out_ref.shape[0]):
        out_ref[copy] = both


def query_kernel(q_ref, gain_ref, out_ref):
    heads, _, head_dim = out_ref.shape
    for head in range(heads):
        raw = q_ref[:, head * head_dim : (head + 1) * head_dim].astype(jnp.float32)
        mean = jnp.mean(raw * raw, axis=-1, keepdims=True)
        out_ref[head] = (raw * lax.rsqrt(mean + EPS) * gain_ref[...]).astype(out_ref.dtype)


def attend_kernel(
    image_start_ref,
    slot_image_ref,
    place_ref,
    q_ref,
    kv_ref,
    out_ref,
    keys_ref,
    values_ref,
    begin_ref,
    total_ref,
    *,
    scale,
    group,
    slots_here,
):
    slots, tile_rows, width = kv_ref.shape
    heads, tokens, head_dim = q_ref.shape
    members, own, _ = out_ref.shape
    n_images = image_start_ref.shape[0]
    plane_rank = place_ref[0]
    member = place_ref[1]
    first_token = plane_rank * tokens
    total_tokens = (slots // slots_here) * tokens
    limit = first_token + tokens
    ones = jnp.ones((tile_rows, head_dim), jnp.bfloat16)

    def take(place, kept):
        rank = place // slots_here
        slot = (rank * PLANE + member) * slots_here + place % slots_here
        image = slot_image_ref[slot]
        start = image_start_ref[jnp.minimum(image, n_images - 1)]
        begin = jnp.where(image < n_images, start, total_tokens)

        @pl.when(begin < limit)
        def _():
            keys_ref[kept] = kv_ref[place, :, :head_dim]
            values_ref[kept] = jnp.concatenate([kv_ref[place, :, head_dim:], ones], axis=1)
            begin_ref[kept] = begin

        return kept + (begin < limit).astype(jnp.int32)

    kept = lax.fori_loop(0, slots, take, jnp.int32(0))
    turns = (kept + group - 1) // group

    def fill(place, _):
        keys_ref[place] = kv_ref[0, :, :head_dim]
        values_ref[place] = jnp.concatenate([kv_ref[0, :, head_dim:], ones], axis=1)
        begin_ref[place] = total_tokens
        return 0

    lax.fori_loop(kept, turns * group, fill, 0)
    total_ref[...] = jnp.zeros_like(total_ref)

    count = group * tile_rows
    lane = lax.broadcasted_iota(jnp.int32, (1, count), 1)
    position = first_token + lax.broadcasted_iota(jnp.int32, (tokens, 1), 0)

    def turn(number, _):
        base = number * group
        row_begin = jnp.zeros((1, count), jnp.int32)
        for place in range(group):
            row_begin = jnp.where(lane >= place * tile_rows, begin_ref[base + place], row_begin)
        keys = keys_ref[pl.ds(base, group)].reshape(count, head_dim)
        values = values_ref[pl.ds(base, group)].reshape(count, 2 * head_dim)
        visible = row_begin <= position

        def one_head(head, _):
            scores = lax.dot_general(
                q_ref[head],
                keys,
                (((1,), (1,)), ((), ())),
                preferred_element_type=jnp.float32,
            )
            weights = jnp.where(visible, jnp.exp2(scores * scale), 0.0)
            total_ref[head] += jnp.dot(
                weights.astype(jnp.bfloat16), values, preferred_element_type=jnp.float32
            )
            return 0

        lax.fori_loop(0, heads, one_head, 0)
        return 0

    lax.fori_loop(0, turns, turn, 0)

    column = lax.broadcasted_iota(jnp.int32, (own, head_dim), 1)
    for to in range(members):
        rows = slice(to * own, (to + 1) * own)
        sums = jnp.zeros((own, head_dim), jnp.float32)
        for head in range(heads):
            columns = slice(head * head_dim, (head + 1) * head_dim)
            out_ref[to, :, columns] = total_ref[head, rows, :head_dim].astype(out_ref.dtype)
            denom = total_ref[head, rows, head_dim:]
            high = denom.astype(jnp.bfloat16).astype(jnp.float32)
            sums = jnp.where(column == head, high, sums)
            sums = jnp.where(column == heads + head, denom - high, sums)
        out_ref[to, :, heads * head_dim :] = sums.astype(out_ref.dtype)


def combine_kernel(image_start_ref, place_ref, gate_ref, parts_ref, out_ref):
    members, own, width = parts_ref.shape
    plane_rank = place_ref[0]
    member = place_ref[1]
    out_width = out_ref.shape[1]
    head_dim = width - out_width
    heads = out_width // head_dim
    first = (plane_rank * members + member) * own
    position = first + lax.broadcasted_iota(jnp.int32, (own, 1), 0)
    seen = position >= image_start_ref[0]
    factor = jnp.tanh(gate_ref[...])
    sums = jnp.sum(parts_ref[:, :, out_width:].astype(jnp.float32), axis=0)
    for head in range(heads):
        columns = slice(head * head_dim, (head + 1) * head_dim)
        denom = sums[:, head : head + 1] + sums[:, heads + head : heads + head + 1]
        safe = jnp.where(seen, denom, 1.0)
        numer = jnp.sum(parts_ref[:, :, columns].astype(jnp.float32), axis=0)
        out_ref[:, columns] = jnp.where(seen, factor * numer / safe, 0.0).astype(out_ref.dtype)


def local(
    queries,
    q_gain,
    k_gain,
    attn_gate,
    vision,
    key_projection_matrix,
    value_projection_matrix,
    image_start,
    slot_image,
):
    ctx_size = lax.axis_size("ctx")
    head_size = lax.axis_size("head")
    ranks = ctx_size // PLANE
    own_index = lax.axis_index("ctx")
    plane_rank = own_index // PLANE
    member = own_index % PLANE
    place = jnp.stack([plane_rank, member]).astype(jnp.int32)
    head_dim = q_gain.shape[0]
    tokens, q_cols = queries.shape
    heads = q_cols // head_dim
    rows, features = vision.shape
    piece_rows, kv_cols = key_projection_matrix.shape
    along_z = [[rank * PLANE + m for rank in range(ranks)] for m in range(PLANE)]
    in_plane = [[rank * PLANE + m for m in range(PLANE)] for rank in range(ranks)]
    whole_plane = [
        [rank * PLANE * head_size + i for i in range(PLANE * head_size)] for rank in range(ranks)
    ]

    with jax.named_scope("gather_queries"):
        all_queries = lax.all_gather(
            queries, "ctx", axis_index_groups=in_plane, axis=0, tiled=True
        )

    with jax.named_scope("gather_projections"):
        weights = jnp.concatenate([key_projection_matrix, value_projection_matrix], axis=1)
        weights = jnp.broadcast_to(weights[None], (ranks,) + weights.shape)
        weights = lax.all_to_all(weights, "ctx", 0, 0, axis_index_groups=along_z)

    with jax.named_scope("spread_vision"):
        blocks = features // (piece_rows * PLANE)
        mine = vision.reshape(rows, blocks, PLANE, piece_rows).transpose(2, 0, 1, 3)
        mine = mine.reshape(PLANE, 1, rows, blocks * piece_rows)
        mine = jnp.broadcast_to(mine, (PLANE, head_size, rows, blocks * piece_rows))
        mine = mine.reshape(PLANE * head_size, rows, blocks * piece_rows)
        spread = lax.all_to_all(mine, ("ctx", "head"), 0, 0, axis_index_groups=whole_plane)

    with jax.named_scope("project"):
        partial = pl.pallas_call(
            project_kernel,
            out_shape=jax.ShapeDtypeStruct((PLANE, rows, 2 * kv_cols), jnp.bfloat16),
            in_specs=[vmem(), vmem()],
            out_specs=vmem(),
            compiler_params=params(),
        )(
            spread.reshape(PLANE, head_size, rows, blocks * piece_rows),
            weights.reshape(head_size, blocks * piece_rows, 2 * kv_cols),
        )

    with jax.named_scope("sum_projections"):
        partial = lax.all_to_all(partial, "ctx", 0, 0, axis_index_groups=in_plane)
        own_kv = pl.pallas_call(
            finish_kernel,
            out_shape=jax.ShapeDtypeStruct((ranks, rows, 2 * kv_cols), jnp.bfloat16),
            in_specs=[vmem(), vmem()],
            out_specs=vmem(),
            compiler_params=params(),
        )(partial, k_gain.reshape(1, head_dim))

    with jax.named_scope("gather_keys_values"):
        all_kv = lax.all_to_all(own_kv, "ctx", 0, 0, axis_index_groups=along_z)

    with jax.named_scope("norm_queries"):
        normed = pl.pallas_call(
            query_kernel,
            out_shape=jax.ShapeDtypeStruct((heads, PLANE * tokens, head_dim), jnp.bfloat16),
            in_specs=[vmem(), vmem()],
            out_specs=vmem(),
            compiler_params=params(),
        )(all_queries, q_gain.reshape(1, head_dim))

    with jax.named_scope("attend"):
        slots_here = slot_image.shape[0] // ctx_size
        tile_rows = rows // slots_here
        slots = ranks * slots_here
        group = math.gcd(slots, 8)
        packed = pl.pallas_call(
            functools.partial(
                attend_kernel,
                scale=head_dim ** (-0.5) * math.log2(math.e),
                group=group,
                slots_here=slots_here,
            ),
            out_shape=jax.ShapeDtypeStruct((PLANE, tokens, q_cols + head_dim), jnp.bfloat16),
            in_specs=[smem(), smem(), smem(), vmem(), vmem()],
            out_specs=vmem(),
            scratch_shapes=[
                pltpu.VMEM((slots, tile_rows, head_dim), jnp.bfloat16),
                pltpu.VMEM((slots, tile_rows, 2 * head_dim), jnp.bfloat16),
                pltpu.SMEM((slots,), jnp.int32),
                pltpu.VMEM((heads, PLANE * tokens, 2 * head_dim), jnp.float32),
            ],
            compiler_params=params(),
        )(
            image_start,
            slot_image,
            place,
            normed,
            all_kv.reshape(slots, tile_rows, 2 * kv_cols),
        )

    with jax.named_scope("sum_attention"):
        packed = lax.all_to_all(packed, "ctx", 0, 0, axis_index_groups=in_plane)
        return pl.pallas_call(
            combine_kernel,
            out_shape=jax.ShapeDtypeStruct((tokens, q_cols), jnp.bfloat16),
            in_specs=[smem(), smem(), vmem(), vmem()],
            out_specs=vmem(),
            compiler_params=params(),
        )(image_start, place, attn_gate.reshape(1, 1), packed)


def solution(mesh):
    in_specs = (
        P("ctx", "head"),
        P(),
        P(),
        P(),
        P("ctx", "head"),
        P("ctx", "head"),
        P("ctx", "head"),
        P(),
        P(),
    )
    out_specs = P("ctx", "head")
    return jax.shard_map(local, mesh=mesh, in_specs=in_specs, out_specs=out_specs, check_vma=False)
```

time: 702 us -> 223 us (0.32)
  the two profiles are of different devices: /device:TPU:1 before, /device:TPU:488 now
where the time goes in v1:
time: 223 us
  waiting for transfers between devices  95.9 us (43%)
  blocking collectives  71.2 us (32%)
  Pallas kernels  20.6 us (9%)
  starting transfers between devices  16.5 us (7%)
  between operations  14.2 us (6%)
  local copies, waits for them, and re-layouts  4.2 us (2%)
    all_to_all x1, blocking collectives, local(): weights = lax.all_to_all(weights, 'ctx', 0, 0, axis_index_groups=along_z)  61.2 us
    all_to_all x1, waiting for transfers between devices, local(): lax.all_to_all(mine, ('ctx', 'head'), 0, 0, axis_index_groups=whole_plane)  29 us
    all_gather x1, waiting for transfers between devices, local(): lax.all_gather(queries, 'ctx', axis_index_groups=in_plane, axis=0, tiled=...  29 us
    all_to_all x1, waiting for transfers between devices, local(): all_kv = lax.all_to_all(own_kv, 'ctx', 0, 0, axis_index_groups=along_z)  20.6 us
    all_to_all x1, waiting for transfers between devices, local(): packed = lax.all_to_all(packed, 'ctx', 0, 0, axis_index_groups=in_plane)  16.7 us
    pallas_call x1, Pallas kernels, local(): pl.pallas_call(functools.partial(attend_kernel, scale=head_dim ** (-0.5)...  16.6 us
    all_to_all x1, blocking collectives, local(): partial = lax.all_to_all(partial, 'ctx', 0, 0, axis_index_groups=in_plane)  9.93 us
    all_to_all x1, starting transfers between devices, local(): lax.all_to_all(mine, ('ctx', 'head'), 0, 0, axis_index_groups=whole_plane)  7.66 us
  transfers between devices with their start and end apart: 4, of which 4 were waited for; matrix products, arithmetic and copies ran while one was open for 0% of the time, Pallas kernels for 0%

profile of v1, /device:TPU:488, one launch (start us, length us, event | category | flops | bytes accessed | tf_op | source)
XLA Modules:
  0.0 222.6 jit_solution(3062793268445585903)
XLA Ops:
  6.5 1.1 copy.11
  7.7 0.1 copy.13
  7.8 1.6 broadcast_in_dim.14
  9.4 0.0 copy-start.5
  9.4 0.0 copy-start.6
  9.4 7.7 %all-to-all-start = ((bf16[32,128,256]{2,1,0:T(8,128)(2,1)}), bf16[32,128,256]{2,1,0:T(8,128)(2,1)S(1)}, u32[]{:S(2)}, u32[]{:S(2)}) async-start(bf16[32,128,256]{2,1,0:T(8,128)(2,1)} %bitcast.19), calls=%async_computation | async-start | bytes 4194304 | tf_op jit(solution)/shard_map/spread_vision/all_to_all | solution.py:224
  17.1 0.0 copy-done.5
  17.1 0.0 copy-done.6
  17.1 29.0 %all-to-all-done = bf16[32,128,256]{2,1,0:T(8,128)(2,1)S(1)} async-done(((bf16[32,128,256]{2,1,0:T(8,128)(2,1)}), bf16[32,128,256]{2,1,0:T(8,128)(2,1)S(1)}, u32[]{:S(2)}, u32[]{:S(2)}) %all-to-all-start) | async-done | bytes 2097184 | tf_op jit(solution)/shard_map/spread_vision/all_to_all | solution.py:224
  46.1 0.1 broadcast_in_dim.15
  46.2 61.2 %all_to_all.25 = bf16[16,128,256]{2,1,0:T(8,128)(2,1)S(1)} all-to-all(bf16[16,128,256]{2,1,0:T(8,128)(2,1)S(1)} %broadcast_in_dim.15), channel_id=1, replica_groups={{0,32,64,96,128,160,192,224,256,288,320,352,384,416,448,480},{8,40,72,1..., dimensions={0} | all-to-all | bytes 2097152 | tf_op jit(solution)/shard_map/gather_projections/all_to_all | solution.py:216
  107.5 0.0 copy-start.2
  107.5 0.7 project.1
  108.2 0.0 copy-start.3
  108.2 9.9 %all_to_all.26.parts_ref = bf16[4,128,256]{2,1,0:T(8,128)(2,1)S(1)} all-to-all(bf16[4,128,256]{2,1,0:T(8,128)(2,1)S(1)} %project.1), channel_id=1, replica_groups={{0,8,16,24},{32,40,48,56},{64,72,80,88},{96,104,112,120},{128,136,144,1..., dimensions={0} | all-to-all | bytes 524288 | tf_op jit(solution)/shard_map/sum_projections/all_to_all | solution.py:239
  118.1 0.0 copy-done.2
  118.1 1.2 sum_projections.1
  119.3 0.0 copy-start.1
  119.3 0.0 copy-start.4
  119.3 5.2 %all-to-all-start.3 = ((bf16[16,128,256]{2,1,0:T(8,128)(2,1)}), bf16[16,128,256]{2,1,0:T(8,128)(2,1)S(1)}, u32[]{:S(2)}, u32[]{:S(2)}) async-start(bf16[16,128,256]{2,1,0:T(8,128)(2,1)} %sum_projections.1), calls=%async_computation.3 | async-start | bytes 2097152 | tf_op jit(solution)/shard_map/gather_keys_values/all_to_all | solution.py:249
  124.5 0.0 all-gather.2.cloned.1.call-start
  124.6 0.7 all-gather.2.cloned.1.call-update
  125.3 0.1 pad_add_fusion.place_ref
  125.3 29.0 %all-gather.2.cloned.1.call-done.q_ref = bf16[512,1024]{1,0:T(8,128)(2,1)} async-done(((bf16[128,1024]{1,0:T(8,128)(2,1)}), bf16[512,1024]{1,0:T(8,128)(2,1)}) %all-gather.2.cloned.1.call-update) | async-done | bytes 1048592 | tf_op jit(solution)/shard_map/gather_queries/all_gather | solution.py:209
  154.3 0.0 copy-done.3
  154.3 0.0 copy-start
  154.3 1.2 copy-done
  155.5 0.6 norm_queries.1.q_ref
  156.2 20.6 %all-to-all-done.3 = bf16[16,128,256]{2,1,0:T(8,128)(2,1)S(1)} async-done(((bf16[16,128,256]{2,1,0:T(8,128)(2,1)}), bf16[16,128,256]{2,1,0:T(8,128)(2,1)S(1)}, u32[]{:S(2)}, u32[]{:S(2)}) %all-to-all-start.3) | async-done | bytes 1048608 | tf_op jit(solution)/shard_map/gather_keys_values/all_to_all | solution.py:249
  176.8 0.0 copy-done.1
  176.8 0.0 copy-done.4
  176.8 16.6 %attend.1 = bf16[4,128,1152]{2,1,0:T(8,128)(2,1)} custom-call(s32[24]{0:T(128)S(1)} %copy-done.1, s32[128]{0:T(128)S(1)} %copy-done.4, s32[2]{0:T(128)S(1)} %pad_add_fusion.place_ref, bf16[8,512,128]{2,1,0:T(8,128)(2,1)S(1)} %norm_queries.1.q_ref, bf16[32,64,256]{2,1,0:T(8,128)(2,1)S(1)} %bitcast.15), custom_call_target="tpu_custom_call" | custom-call | tf_op jit(solution)/shard_map/attend/pallas_call | solution.py:265
  193.4 3.5 %all-to-all-start.4 = ((bf16[4,128,1152]{2,1,0:T(8,128)(2,1)}), bf16[4,128,1152]{2,1,0:T(8,128)(2,1)S(1)}, u32[]{:S(2)}, u32[]{:S(2)}) async-start(bf16[4,128,1152]{2,1,0:T(8,128)(2,1)} %attend.1), calls=%async_computation.4 | async-start | bytes 2359296 | tf_op jit(solution)/shard_map/sum_attention/all_to_all | solution.py:291
  197.6 16.7 %all-to-all-done.4.parts_ref = bf16[4,128,1152]{2,1,0:T(8,128)(2,1)S(1)} async-done(((bf16[4,128,1152]{2,1,0:T(8,128)(2,1)}), bf16[4,128,1152]{2,1,0:T(8,128)(2,1)S(1)}, u32[]{:S(2)}, u32[]{:S(2)}) %all-to-all-start.4) | async-done | bytes 1179680 | tf_op jit(solution)/shard_map/sum_attention/all_to_all | solution.py:291
  214.3 1.5 sum_attention.1
  (2 shorter events, 0.0 us)
Async XLA Ops:
  9.4 7.7 %copy-start.5 = (bf16[128,128]{1,0:T(8,128)(2,1)S(1)}, bf16[128,128]{1,0:T(8,128)(2,1)}, u32[]{:S(2)}) copy-start(bf16[128,128]{1,0:T(8,128)(2,1)} %param.15) | copy-start | bytes 98308
  9.4 7.7 %copy-start.6 = (bf16[128,128]{1,0:T(8,128)(2,1)S(1)}, bf16[128,128]{1,0:T(8,128)(2,1)}, u32[]{:S(2)}) copy-start(bf16[128,128]{1,0:T(8,128)(2,1)} %param.14) | copy-start | bytes 98308
  9.4 36.7 %all-to-all-start = ((bf16[32,128,256]{2,1,0:T(8,128)(2,1)}), bf16[32,128,256]{2,1,0:T(8,128)(2,1)S(1)}, u32[]{:S(2)}, u32[]{:S(2)}) async-start(bf16[32,128,256]{2,1,0:T(8,128)(2,1)} %bitcast.19), calls=%async_computation | async-start | bytes 4194304 | tf_op jit(solution)/shard_map/spread_vision/all_to_all | solution.py:224
  107.5 10.7 %copy-start.2 = (f32[128]{0:T(128)S(1)}, f32[128]{0:T(128)}, u32[]{:S(2)}) copy-start(f32[128]{0:T(128)} %param.11) | copy-start | bytes 1540
  108.2 46.1 %copy-start.3 = (f32[128]{0:T(128)S(1)}, f32[128]{0:T(128)}, u32[]{:S(2)}) copy-start(f32[128]{0:T(128)} %param.10) | copy-start | bytes 1540
  119.3 57.5 %copy-start.1 = (s32[24]{0:T(128)S(1)}, s32[24]{0:T(128)}, u32[]{:S(2)}) copy-start(s32[24]{0:T(128)} %image_start_ref.3) | copy-start | bytes 292
  119.3 57.5 %copy-start.4 = (s32[128]{0:T(128)S(1)}, s32[128]{0:T(128)}, u32[]{:S(2)}) copy-start(s32[128]{0:T(128)} %slot_image_ref.1) | copy-start | bytes 1540
  119.3 57.5 %all-to-all-start.3 = ((bf16[16,128,256]{2,1,0:T(8,128)(2,1)}), bf16[16,128,256]{2,1,0:T(8,128)(2,1)S(1)}, u32[]{:S(2)}, u32[]{:S(2)}) async-start(bf16[16,128,256]{2,1,0:T(8,128)(2,1)} %sum_projections.1), calls=%async_computation.3 | async-start | bytes 2097152 | tf_op jit(solution)/shard_map/gather_keys_values/all_to_all | solution.py:249
  124.5 29.8 %all-gather.2.cloned.1.call-start = ((), (), s32[]{:S(2)}) async-start(), calls=%async_computation.5 | async-start | bytes 1310720 | tf_op jit(solution)/shard_map/gather_queries/all_gather | solution.py:209
  154.3 1.2 copy-start
  193.4 20.9 %all-to-all-start.4 = ((bf16[4,128,1152]{2,1,0:T(8,128)(2,1)}), bf16[4,128,1152]{2,1,0:T(8,128)(2,1)S(1)}, u32[]{:S(2)}, u32[]{:S(2)}) async-start(bf16[4,128,1152]{2,1,0:T(8,128)(2,1)} %attend.1), calls=%async_computation.4 | async-start | bytes 2359296 | tf_op jit(solution)/shard_map/sum_attention/all_to_all | solution.py:291
Sparse Core Ops, SparseCore 0:
  127.5 26.8 all-gather.1

commit v2 on v1

--- a/solution.py
+++ b/solution.py
@@ -11,6 +11,7 @@
 EPS = 1e-05
 PLANE = 4
 VMEM_LIMIT = 48 * 1024 * 1024
+OFFSETS = ((-4, 0, 4, 8), (-5, -1, 3, 7), (-3, 1, 5, 9), (-6, -2), (2, 6))
 
 
 def params(**more):
@@ -25,28 +26,47 @@
     return pl.BlockSpec(memory_space=pltpu.SMEM)
 
 
-def project_kernel(x_ref, w_ref, out_ref):
-    members, pieces, rows, depth = x_ref.shape
+def spread_kernel(x_ref, out_ref):
+    members, peers, blocks, _, width = out_ref.shape
+    for member in range(members):
+        for block in range(blocks):
+            first = (block * members + member) * width
+            piece = x_ref[:, first : first + width]
+            for peer in range(peers):
+                out_ref[member, peer, block] = piece
+
+
+def project_kernel(place_ref, x_ref, *refs):
+    weight_refs, out_ref, all_ref = refs[:-2], refs[-2], refs[-1]
+    ranks, depth, width = all_ref.shape
+    members, peers, blocks, rows, _ = x_ref.shape
+    head_dim = width // 2
+    for ref, offsets in zip(weight_refs, OFFSETS):
+        for at, offset in enumerate(offsets):
+            all_ref[lax.rem(place_ref[0] + offset + ranks, ranks)] = ref[at]
     total = None
-    for piece in range(pieces):
-        part = jnp.dot(
-            x_ref[:, piece].reshape(members * rows, depth),
-            w_ref[piece],
-            preferred_element_type=jnp.float32,
-        )
-        total = part if total is None else total + part
-    out_ref[...] = total.reshape(out_ref.shape).astype(out_ref.dtype)
+    for peer in range(peers):
+        for block in range(blocks):
+            part = jnp.dot(
+                x_ref[:, peer, block].reshape(members * rows, depth),
+                all_ref[peer * blocks + block],
+                preferred_element_type=jnp.float32,
+            )
+            total = part if total is None else total + part
+    keys = total[:, :head_dim]
+    high = keys.astype(jnp.bfloat16)
+    low = (keys - high.astype(jnp.float32)).astype(jnp.bfloat16)
+    values = total[:, head_dim:].astype(jnp.bfloat16)
+    out_ref[...] = jnp.concatenate([high, low, values], axis=1).reshape(out_ref.shape)
 
 
 def finish_kernel(parts_ref, gain_ref, out_ref):
     raw = jnp.sum(parts_ref[...].astype(jnp.float32), axis=0)
     head_dim = gain_ref.shape[1]
-    keys = raw[:, :head_dim]
+    keys = raw[:, :head_dim] + raw[:, head_dim : 2 * head_dim]
     mean = jnp.mean(keys * keys, axis=-1, keepdims=True)
     keys = keys * lax.rsqrt(mean + EPS) * gain_ref[...]
-    both = jnp.concatenate([keys, raw[:, head_dim:]], axis=1).astype(out_ref.dtype)
-    for copy in range(out_ref.shape[0]):
-        out_ref[copy] = both
+    out_ref[...] = jnp.concatenate([keys, raw[:, 2 * head_dim :]], axis=1).astype(out_ref.dtype)
 
 
 def query_kernel(q_ref, gain_ref, out_ref):
@@ -62,18 +82,15 @@
     slot_image_ref,
     place_ref,
     q_ref,
-    kv_ref,
-    out_ref,
-    keys_ref,
-    values_ref,
-    begin_ref,
-    total_ref,
-    *,
+    *refs,
     scale,
     group,
     slots_here,
 ):
-    slots, tile_rows, width = kv_ref.shape
+    kv_refs = refs[:-5]
+    out_ref, keys_ref, values_ref, begin_ref, total_ref = refs[-5:]
+    slots, tile_rows, _ = keys_ref.shape
+    ranks = slots // slots_here
     heads, tokens, head_dim = q_ref.shape
     members, own, _ = out_ref.shape
     n_images = image_start_ref.shape[0]
@@ -84,27 +101,32 @@
     limit = first_token + tokens
     ones = jnp.ones((tile_rows, head_dim), jnp.bfloat16)
 
-    def take(place, kept):
-        rank = place // slots_here
-        slot = (rank * PLANE + member) * slots_here + place % slots_here
+    def take_from(kv_ref, at, rank, here, kept):
+        slot = (rank * PLANE + member) * slots_here + here
         image = slot_image_ref[slot]
         start = image_start_ref[jnp.minimum(image, n_images - 1)]
         begin = jnp.where(image < n_images, start, total_tokens)
+        rows = slice(here * tile_rows, (here + 1) * tile_rows)
 
         @pl.when(begin < limit)
         def _():
-            keys_ref[kept] = kv_ref[place, :, :head_dim]
-            values_ref[kept] = jnp.concatenate([kv_ref[place, :, head_dim:], ones], axis=1)
+            keys_ref[kept] = kv_ref[at, rows, :head_dim]
+            values_ref[kept] = jnp.concatenate([kv_ref[at, rows, head_dim:], ones], axis=1)
             begin_ref[kept] = begin
 
         return kept + (begin < limit).astype(jnp.int32)
 
-    kept = lax.fori_loop(0, slots, take, jnp.int32(0))
+    kept = jnp.int32(0)
+    for kv_ref, offsets in zip(kv_refs, OFFSETS):
+        for at, offset in enumerate(offsets):
+            rank = lax.rem(plane_rank + offset + ranks, ranks)
+            for here in range(slots_here):
+                kept = take_from(kv_ref, at, rank, here, kept)
     turns = (kept + group - 1) // group
 
     def fill(place, _):
-        keys_ref[place] = kv_ref[0, :, :head_dim]
-        values_ref[place] = jnp.concatenate([kv_ref[0, :, head_dim:], ones], axis=1)
+        keys_ref[place] = kv_refs[0][0, :tile_rows, :head_dim]
+        values_ref[place] = jnp.concatenate([kv_refs[0][0, :tile_rows, head_dim:], ones], axis=1)
         begin_ref[place] = total_tokens
         return 0
 
@@ -174,6 +196,21 @@
         safe = jnp.where(seen, denom, 1.0)
         numer = jnp.sum(parts_ref[:, :, columns].astype(jnp.float32), axis=0)
         out_ref[:, columns] = jnp.where(seen, factor * numer / safe, 0.0).astype(out_ref.dtype)
+
+
+def gather_along_z(block):
+    ctx_size = lax.axis_size("ctx")
+
+    def shift(value, distance):
+        moved = distance * PLANE
+        return lax.ppermute(
+            value, "ctx", [(i, (i + moved) % ctx_size) for i in range(ctx_size)]
+        )
+
+    block = block[None]
+    own = jnp.concatenate([shift(block, 4), block, shift(block, -4), shift(block, 8)])
+    above, below = shift(own, 1), shift(own, -1)
+    return own, above, below, shift(above[:2], 1), shift(below[1:3], -1)
 
 
 def local(
@@ -199,7 +236,6 @@
     heads = q_cols // head_dim
     rows, features = vision.shape
     piece_rows, kv_cols = key_projection_matrix.shape
-    along_z = [[rank * PLANE + m for rank in range(ranks)] for m in range(PLANE)]
     in_plane = [[rank * PLANE + m for m in range(PLANE)] for rank in range(ranks)]
     whole_plane = [
         [rank * PLANE * head_size + i for i in range(PLANE * head_size)] for rank in range(ranks)
@@ -210,43 +246,25 @@
             queries, "ctx", axis_index_groups=in_plane, axis=0, tiled=True
         )
 
-    with jax.named_scope("gather_projections"):
-        weights = jnp.concatenate([key_projection_matrix, value_projection_matrix], axis=1)
-        weights = jnp.broadcast_to(weights[None], (ranks,) + weights.shape)
-        weights = lax.all_to_all(weights, "ctx", 0, 0, axis_index_groups=along_z)
-
     with jax.named_scope("spread_vision"):
         blocks = features // (piece_rows * PLANE)
-        mine = vision.reshape(rows, blocks, PLANE, piece_rows).transpose(2, 0, 1, 3)
-        mine = mine.reshape(PLANE, 1, rows, blocks * piece_rows)
-        mine = jnp.broadcast_to(mine, (PLANE, head_size, rows, blocks * piece_rows))
-        mine = mine.reshape(PLANE * head_size, rows, blocks * piece_rows)
+        mine = pl.pallas_call(
+            spread_kernel,
+            out_shape=jax.ShapeDtypeStruct(
+                (PLANE, head_size, blocks, rows, piece_rows), jnp.bfloat16
+            ),
+            in_specs=[vmem()],
+            out_specs=vmem(),
+            compiler_params=params(),
+        )(vision)
+        mine = mine.reshape(PLANE * head_size, blocks, rows, piece_rows)
         spread = lax.all_to_all(mine, ("ctx", "head"), 0, 0, axis_index_groups=whole_plane)
-
-    with jax.named_scope("project"):
-        partial = pl.pallas_call(
-            project_kernel,
-            out_shape=jax.ShapeDtypeStruct((PLANE, rows, 2 * kv_cols), jnp.bfloat16),
-            in_specs=[vmem(), vmem()],
-            out_specs=vmem(),
-            compiler_params=params(),
-        )(
-            spread.reshape(PLANE, head_size, rows, blocks * piece_rows),
-            weights.reshape(head_size, blocks * piece_rows, 2 * kv_cols),
+        spread = spread.reshape(PLANE, head_size, blocks, rows, piece_rows)
+
+    with jax.named_scope("gather_projections"):
+        weights = gather_along_z(
+            jnp.concatenate([key_projection_matrix, value_projection_matrix], axis=1)
         )
-
-    with jax.named_scope("sum_projections"):
-        partial = lax.all_to_all(partial, "ctx", 0, 0, axis_index_groups=in_plane)
-        own_kv = pl.pallas_call(
-            finish_kernel,
-            out_shape=jax.ShapeDtypeStruct((ranks, rows, 2 * kv_cols), jnp.bfloat16),
-            in_specs=[vmem(), vmem()],
-            out_specs=vmem(),
-            compiler_params=params(),
-        )(partial, k_gain.reshape(1, head_dim))
-
-    with jax.named_scope("gather_keys_values"):
-        all_kv = lax.all_to_all(own_kv, "ctx", 0, 0, axis_index_groups=along_z)
 
     with jax.named_scope("norm_queries"):
         normed = pl.pallas_call(
@@ -256,6 +274,30 @@
             out_specs=vmem(),
             compiler_params=params(),
         )(all_queries, q_gain.reshape(1, head_dim))
+        spread, normed = lax.optimization_barrier((spread, normed))
+
+    with jax.named_scope("project"):
+        partial = pl.pallas_call(
+            project_kernel,
+            out_shape=jax.ShapeDtypeStruct((PLANE, rows, 3 * kv_cols), jnp.bfloat16),
+            in_specs=[smem()] + [vmem()] * (1 + len(weights)),
+            out_specs=vmem(),
+            scratch_shapes=[pltpu.VMEM((ranks, piece_rows, 2 * kv_cols), jnp.bfloat16)],
+            compiler_params=params(),
+        )(place, spread, *weights)
+
+    with jax.named_scope("sum_projections"):
+        partial = lax.all_to_all(partial, "ctx", 0, 0, axis_index_groups=in_plane)
+        own_kv = pl.pallas_call(
+            finish_kernel,
+            out_shape=jax.ShapeDtypeStruct((rows, 2 * kv_cols), jnp.bfloat16),
+            in_specs=[vmem(), vmem()],
+            out_specs=vmem(),
+            compiler_params=params(),
+        )(partial, k_gain.reshape(1, head_dim))
+
+    with jax.named_scope("gather_keys_values"):
+        all_kv = gather_along_z(own_kv)
 
     with jax.named_scope("attend"):
         slots_here = slot_image.shape[0] // ctx_size
@@ -270,7 +312,7 @@
                 slots_here=slots_here,
             ),
             out_shape=jax.ShapeDtypeStruct((PLANE, tokens, q_cols + head_dim), jnp.bfloat16),
-            in_specs=[smem(), smem(), smem(), vmem(), vmem()],
+            in_specs=[smem()] * 3 + [vmem()] * (1 + len(all_kv)),
             out_specs=vmem(),
             scratch_shapes=[
                 pltpu.VMEM((slots, tile_rows, head_dim), jnp.bfloat16),
@@ -284,7 +326,7 @@
             slot_image,
             place,
             normed,
-            all_kv.reshape(slots, tile_rows, 2 * kv_cols),
+            *all_kv,
         )
 
     with jax.named_scope("sum_attention"):

time: 223 us -> 173 us (0.78)
  the two profiles are of different devices: /device:TPU:488 before, /device:TPU:1 now
where the time goes in v2:
time: 173 us; the launch traced here: 170 us
  starting transfers between devices  85.1 us (49%)
  waiting for transfers between devices  35.9 us (21%)
  blocking collectives  15.3 us (9%)
  between operations  14.4 us (8%)
  Pallas kernels  12.1 us (7%)
  local copies, waits for them, and re-layouts  6.91 us (4%)
    ppermute x14, starting transfers between devices, shift(): lax.ppermute(value, 'ctx', [(i, (i + moved) % ctx_size) for i in range(ct...  67.7 us
    ppermute x14, waiting for transfers between devices, shift(): lax.ppermute(value, 'ctx', [(i, (i + moved) % ctx_size) for i in range(ct...  19.3 us
    all_to_all x1, waiting for transfers between devices, local(): packed = lax.all_to_all(packed, 'ctx', 0, 0, axis_index_groups=in_plane)  15.9 us
    all_to_all x1, blocking collectives, local(): partial = lax.all_to_all(partial, 'ctx', 0, 0, axis_index_groups=in_plane)  15.3 us
    all_to_all x1, starting transfers between devices, local(): lax.all_to_all(mine, ('ctx', 'head'), 0, 0, axis_index_groups=whole_plane)  10.7 us
    pallas_call x1, Pallas kernels, local(): pl.pallas_call(functools.partial(attend_kernel, scale=head_dim ** (-0.5)...  7.3 us
    all_to_all x1, starting transfers between devices, local(): packed = lax.all_to_all(packed, 'ctx', 0, 0, axis_index_groups=in_plane)  6.69 us
    unnamed x26, local copies, waits for them, and re-layouts  5.48 us
  transfers between devices with their start and end apart: 17, of which 10 were waited for; matrix products, arithmetic and copies ran while one was open for 1% of the time, Pallas kernels for 0%

profile of v2, /device:TPU:1, one launch (start us, length us, event | category | flops | bytes accessed | tf_op | source)
XLA Modules:
  0.0 169.9 jit_solution(4727614251400371967)
XLA Ops:
  6.5 0.9 copy-done.6
  7.5 0.3 spread_vision.1
  7.8 1.3 copy-done
  9.1 10.7 %all-to-all-start = ((bf16[32,2,128,128]{3,2,1,0:T(8,128)(2,1)}), bf16[32,2,128,128]{3,2,1,0:T(8,128)(2,1)S(1)}, u32[]{:S(2)}, u32[]{:S(2)}) async-start(bf16[32,2,128,128]{3,2,1,0:T(8,128)(2,1)} %bitcast.12), calls=%async_computation | async-start | bytes 4194304 | tf_op jit(solution)/shard_map/spread_vision/all_to_all | solution.py:261
  19.8 0.0 all-gather.2.cloned.1.call-start
  19.9 0.7 all-gather.2.cloned.1.call-update
  20.6 13.4 %collective-permute-start.2 = (bf16[1,128,256]{2,1,0:T(8,128)(2,1)S(1)}, bf16[1,128,256]{2,1,0:T(8,128)(2,1)S(1)}, u32[]{:S(2)}, u32[]{:S(2)}) collective-permute-start(bf16[1,128,256]{2,1,0:T(8,128)(2,1)S(1)} %maximum_bitcast_fusion), channel_id=1, source_target_pairs={{0,256},{8,264},{16,272},{24,280},{32,288},{40,296},{48,304},{56,3... | collective-permute-start | bytes 196616 | tf_op jit(solution)/shard_map/gather_projections/ppermute | solution.py:206
  34.1 1.9 %collective-permute-start.1 = (bf16[1,128,256]{2,1,0:T(8,128)(2,1)S(1)}, bf16[1,128,256]{2,1,0:T(8,128)(2,1)S(1)}, u32[]{:S(2)}, u32[]{:S(2)}) collective-permute-start(bf16[1,128,256]{2,1,0:T(8,128)(2,1)S(1)} %maximum_bitcast_fusion), channel_id=1, source_target_pairs={{0,384},{8,392},{16,400},{24,408},{32,416},{40,424},{48,432},{56,4... | collective-permute-start | bytes 196616 | tf_op jit(solution)/shard_map/gather_projections/ppermute | solution.py:206
  36.0 7.3 %collective-permute-start = (bf16[1,128,256]{2,1,0:T(8,128)(2,1)S(1)}, bf16[1,128,256]{2,1,0:T(8,128)(2,1)S(1)}, u32[]{:S(2)}, u32[]{:S(2)}) collective-permute-start(bf16[1,128,256]{2,1,0:T(8,128)(2,1)S(1)} %maximum_bitcast_fusion), channel_id=1, source_target_pairs={{0,128},{8,136},{16,144},{24,152},{32,160},{40,168},{48,176},{56,1... | collective-permute-start | bytes 196616 | tf_op jit(solution)/shard_map/gather_projections/ppermute | solution.py:206
  43.3 0.0 collective-permute-done.2
  43.3 1.8 %collective-permute-done.1 = bf16[1,128,256]{2,1,0:T(8,128)(2,1)S(1)} collective-permute-done((bf16[1,128,256]{2,1,0:T(8,128)(2,1)S(1)}, bf16[1,128,256]{2,1,0:T(8,128)(2,1)S(1)}, u32[]{:S(2)}, u32[]{:S(2)}) %collective-permute-start.1) | collective-permute-done | bytes 65568 | tf_op jit(solution)/shard_map/gather_projections/ppermute | solution.py:206
  45.1 1.9 %collective-permute-done = bf16[1,128,256]{2,1,0:T(8,128)(2,1)S(1)} collective-permute-done((bf16[1,128,256]{2,1,0:T(8,128)(2,1)S(1)}, bf16[1,128,256]{2,1,0:T(8,128)(2,1)S(1)}, u32[]{:S(2)}, u32[]{:S(2)}) %collective-permute-start) | collective-permute-done | bytes 65568 | tf_op jit(solution)/shard_map/gather_projections/ppermute | solution.py:206
  47.0 4.1 %collective-permute-start.3 = (bf16[4,128,256]{2,1,0:T(8,128)(2,1)S(1)}, bf16[4,128,256]{2,1,0:T(8,128)(2,1)S(1)}, u32[]{:S(2)}, u32[]{:S(2)}) collective-permute-start(bf16[4,128,256]{2,1,0:T(8,128)(2,1)S(1)} %pad_maximum_fusion.refs_0_), channel_id=1, source_target_pairs={{0,32},{8,40},{16,48},{24,56},{32,64},{40,72},{48,80},{56,88},{64,... | collective-permute-start | bytes 786440 | tf_op jit(solution)/shard_map/gather_projections/ppermute | solution.py:206
  51.1 3.2 %collective-permute-start.4 = (bf16[4,128,256]{2,1,0:T(8,128)(2,1)S(1)}, bf16[4,128,256]{2,1,0:T(8,128)(2,1)S(1)}, u32[]{:S(2)}, u32[]{:S(2)}) collective-permute-start(bf16[4,128,256]{2,1,0:T(8,128)(2,1)S(1)} %pad_maximum_fusion.refs_0_), channel_id=1, source_target_pairs={{0,480},{8,488},{16,496},{24,504},{32,0},{40,8},{48,16},{56,24},{6... | collective-permute-start | bytes 786440 | tf_op jit(solution)/shard_map/gather_projections/ppermute | solution.py:206
  54.3 3.0 %collective-permute-done.3.refs_1_ = bf16[4,128,256]{2,1,0:T(8,128)(2,1)S(1)} collective-permute-done((bf16[4,128,256]{2,1,0:T(8,128)(2,1)S(1)}, bf16[4,128,256]{2,1,0:T(8,128)(2,1)S(1)}, u32[]{:S(2)}, u32[]{:S(2)}) %collective-permute-start.3) | collective-permute-done | bytes 262176 | tf_op jit(solution)/shard_map/gather_projections/ppermute | solution.py:206
  57.2 0.7 slice.16
  57.9 2.8 %collective-permute-start.5 = (bf16[2,128,256]{2,1,0:T(8,128)(2,1)}, bf16[2,128,256]{2,1,0:T(8,128)(2,1)S(1)}, u32[]{:S(2)}, u32[]{:S(2)}) collective-permute-start(bf16[2,128,256]{2,1,0:T(8,128)(2,1)} %slice.16), channel_id=1, source_target_pairs={{0,32},{8,40},{16,48},{24,56},{32,64},{40,72},{48,80},{56,88},{64,... | collective-permute-start | bytes 393224 | tf_op jit(solution)/shard_map/gather_projections/ppermute | solution.py:206
  60.8 0.7 slice.17
  61.5 0.0 copy-done.4
  61.5 3.7 %collective-permute-start.6 = (bf16[2,128,256]{2,1,0:T(8,128)(2,1)}, bf16[2,128,256]{2,1,0:T(8,128)(2,1)}, u32[]{:S(2)}, u32[]{:S(2)}) collective-permute-start(bf16[2,128,256]{2,1,0:T(8,128)(2,1)} %slice.17), channel_id=1, source_target_pairs={{0,480},{8,488},{16,496},{24,504},{32,0},{40,8},{48,16},{56,24},{6... | collective-permute-start | bytes 393224 | tf_op jit(solution)/shard_map/gather_projections/ppermute | solution.py:206
  65.2 0.1 pad_add_fusion.place_ref
  65.3 1.2 copy-done.1
  66.5 0.6 norm_queries.1.q_ref
  67.1 0.0 copy-start.10
  67.2 0.0 copy-start.7
  67.2 0.0 copy-start.9
  67.2 0.5 collective-permute-done.6.refs_4_
  67.7 0.9 copy-done.3
  68.6 0.9 copy-done.5
  69.6 2.2 %project.1 = bf16[4,128,384]{2,1,0:T(8,128)(2,1)S(1)} custom-call(s32[2]{0:T(128)S(1)} %pad_add_fusion.place_ref, bf16[4,8,2,128,128]{4,3,2,1,0:T(8,128)(2,1)S(1)} %bitcast.11, bf16[4,128,256]{2,1,0:T(8,128)(2,1)S(1)} %pad_maximum_fusion.refs_0_, bf16[4,128,256]{2,1,0:T(8,128)(2,1)S(1)} %copy-done.3, bf16[4,128,256]{2,1,0:T(8,128)(2,1)S(1)} %copy-done.5, ...), custom_call_target="tpu_custom_call" | custom-call | tf_op jit(solution)/shard_map/project/pallas_call | solution.py:280
  71.8 15.3 %all_to_all.15.parts_ref = bf16[4,128,384]{2,1,0:T(8,128)(2,1)S(1)} all-to-all(bf16[4,128,384]{2,1,0:T(8,128)(2,1)S(1)} %project.1), channel_id=1, replica_groups={{0,8,16,24},{32,40,48,56},{64,72,80,88},{96,104,112,120},{128,136,144,1..., dimensions={0} | all-to-all | bytes 786432 | tf_op jit(solution)/shard_map/sum_projections/all_to_all | solution.py:290
  87.2 0.1 sum_projections.1
  87.3 8.5 %collective-permute-start.9 = (bf16[1,128,256]{2,1,0:T(8,128)(2,1)S(1)}, bf16[1,128,256]{2,1,0:T(8,128)(2,1)S(1)}, u32[]{:S(2)}, u32[]{:S(2)}) collective-permute-start(bf16[1,128,256]{2,1,0:T(8,128)(2,1)S(1)} %bitcast.13), channel_id=1, source_target_pairs={{0,256},{8,264},{16,272},{24,280},{32,288},{40,296},{48,304},{56,3... | collective-permute-start | bytes 196616 | tf_op jit(solution)/shard_map/gather_keys_values/ppermute | solution.py:206
  95.8 5.6 %collective-permute-start.8 = (bf16[1,128,256]{2,1,0:T(8,128)(2,1)S(1)}, bf16[1,128,256]{2,1,0:T(8,128)(2,1)S(1)}, u32[]{:S(2)}, u32[]{:S(2)}) collective-permute-start(bf16[1,128,256]{2,1,0:T(8,128)(2,1)S(1)} %bitcast.14), channel_id=1, source_target_pairs={{0,384},{8,392},{16,400},{24,408},{32,416},{40,424},{48,432},{56,4... | collective-permute-start | bytes 196616 | tf_op jit(solution)/shard_map/gather_keys_values/ppermute | solution.py:206
  101.4 3.6 %collective-permute-start.7 = (bf16[1,128,256]{2,1,0:T(8,128)(2,1)S(1)}, bf16[1,128,256]{2,1,0:T(8,128)(2,1)S(1)}, u32[]{:S(2)}, u32[]{:S(2)}) collective-permute-start(bf16[1,128,256]{2,1,0:T(8,128)(2,1)S(1)} %bitcast.15), channel_id=1, source_target_pairs={{0,128},{8,136},{16,144},{24,152},{32,160},{40,168},{48,176},{56,1... | collective-permute-start | bytes 196616 | tf_op jit(solution)/shard_map/gather_keys_values/ppermute | solution.py:206
  105.0 0.9 collective-permute-done.8
  105.8 4.6 %collective-permute-done.7 = bf16[1,128,256]{2,1,0:T(8,128)(2,1)S(1)} collective-permute-done((bf16[1,128,256]{2,1,0:T(8,128)(2,1)S(1)}, bf16[1,128,256]{2,1,0:T(8,128)(2,1)S(1)}, u32[]{:S(2)}, u32[]{:S(2)}) %collective-permute-start.7) | collective-permute-done | bytes 65568 | tf_op jit(solution)/shard_map/gather_keys_values/ppermute | solution.py:206
  110.5 1.9 %collective-permute-start.10 = (bf16[4,128,256]{2,1,0:T(8,128)(2,1)S(1)}, bf16[4,128,256]{2,1,0:T(8,128)(2,1)S(1)}, u32[]{:S(2)}, u32[]{:S(2)}) collective-permute-start(bf16[4,128,256]{2,1,0:T(8,128)(2,1)S(1)} %pad_maximum_fusion.1.refs_0_), channel_id=1, source_target_pairs={{0,32},{8,40},{16,48},{24,56},{32,64},{40,72},{48,80},{56,88},{64,... | collective-permute-start | bytes 786440 | tf_op jit(solution)/shard_map/gather_keys_values/ppermute | solution.py:206
  112.4 5.3 %collective-permute-start.11 = (bf16[4,128,256]{2,1,0:T(8,128)(2,1)S(1)}, bf16[4,128,256]{2,1,0:T(8,128)(2,1)S(1)}, u32[]{:S(2)}, u32[]{:S(2)}) collective-permute-start(bf16[4,128,256]{2,1,0:T(8,128)(2,1)S(1)} %pad_maximum_fusion.1.refs_0_), channel_id=1, source_target_pairs={{0,480},{8,488},{16,496},{24,504},{32,0},{40,8},{48,16},{56,24},{6... | collective-permute-start | bytes 786440 | tf_op jit(solution)/shard_map/gather_keys_values/ppermute | solution.py:206
  117.7 1.8 %collective-permute-done.10.refs_1_ = bf16[4,128,256]{2,1,0:T(8,128)(2,1)S(1)} collective-permute-done((bf16[4,128,256]{2,1,0:T(8,128)(2,1)S(1)}, bf16[4,128,256]{2,1,0:T(8,128)(2,1)S(1)}, u32[]{:S(2)}, u32[]{:S(2)}) %collective-permute-start.10) | collective-permute-done | bytes 262176 | tf_op jit(solution)/shard_map/gather_keys_values/ppermute | solution.py:206
  119.6 1.9 %collective-permute-start.12 = (bf16[2,128,256]{2,1,0:T(8,128)(2,1)S(1)}, bf16[2,128,256]{2,1,0:T(8,128)(2,1)S(1)}, u32[]{:S(2)}, u32[]{:S(2)}) collective-permute-start(bf16[2,128,256]{2,1,0:T(8,128)(2,1)S(1)} %slice.18), channel_id=1, source_target_pairs={{0,32},{8,40},{16,48},{24,56},{32,64},{40,72},{48,80},{56,88},{64,... | collective-permute-start | bytes 393224 | tf_op jit(solution)/shard_map/gather_keys_values/ppermute | solution.py:206
  121.5 4.6 %collective-permute-start.13 = (bf16[2,128,256]{2,1,0:T(8,128)(2,1)S(1)}, bf16[2,128,256]{2,1,0:T(8,128)(2,1)S(1)}, u32[]{:S(2)}, u32[]{:S(2)}) collective-permute-start(bf16[2,128,256]{2,1,0:T(8,128)(2,1)S(1)} %slice.19), channel_id=1, source_target_pairs={{0,480},{8,488},{16,496},{24,504},{32,0},{40,8},{48,16},{56,24},{6... | collective-permute-start | bytes 393224 | tf_op jit(solution)/shard_map/gather_keys_values/ppermute | solution.py:206
  126.1 0.4 collective-permute-done.12.refs_3_
  126.5 4.5 %collective-permute-done.13.refs_4_ = bf16[2,128,256]{2,1,0:T(8,128)(2,1)S(1)} collective-permute-done((bf16[2,128,256]{2,1,0:T(8,128)(2,1)S(1)}, bf16[2,128,256]{2,1,0:T(8,128)(2,1)S(1)}, u32[]{:S(2)}, u32[]{:S(2)}) %collective-permute-start.13) | collective-permute-done | bytes 131104 | tf_op jit(solution)/shard_map/gather_keys_values/ppermute | solution.py:206
  131.0 7.3 %attend.1 = bf16[4,128,1152]{2,1,0:T(8,128)(2,1)} custom-call(s32[24]{0:T(128)S(1)} %copy-done.7, s32[128]{0:T(128)S(1)} %copy-done.9, s32[2]{0:T(128)S(1)} %pad_add_fusion.place_ref, bf16[8,512,128]{2,1,0:T(8,128)(2,1)S(1)} %norm_queries.1.q_ref, bf16[4,128,256]{2,1,0:T(8,128)(2,1)S(1)} %pad_maximum_fusion.1.refs_0_, ...), custom_call_target="tpu_custom_call" | custom-call | tf_op jit(solution)/shard_map/attend/pallas_call | solution.py:307
  138.3 6.7 %all-to-all-start.2 = ((bf16[4,128,1152]{2,1,0:T(8,128)(2,1)}), bf16[4,128,1152]{2,1,0:T(8,128)(2,1)S(1)}, u32[]{:S(2)}, u32[]{:S(2)}) async-start(bf16[4,128,1152]{2,1,0:T(8,128)(2,1)} %attend.1), calls=%async_computation.2 | async-start | bytes 2359296 | tf_op jit(solution)/shard_map/sum_attention/all_to_all | solution.py:333
  145.6 15.9 %all-to-all-done.2.parts_ref = bf16[4,128,1152]{2,1,0:T(8,128)(2,1)S(1)} async-done(((bf16[4,128,1152]{2,1,0:T(8,128)(2,1)}), bf16[4,128,1152]{2,1,0:T(8,128)(2,1)S(1)}, u32[]{:S(2)}, u32[]{:S(2)}) %all-to-all-start.2) | async-done | bytes 1179680 | tf_op jit(solution)/shard_map/sum_attention/all_to_all | solution.py:333
  161.5 1.5 sum_attention.1
  (28 shorter events, 0.1 us)
Async XLA Ops:
  6.5 0.9 copy-start.6
  7.8 1.4 copy-start
  9.1 11.5 %copy-start.11 = (bf16[128,128]{1,0:T(8,128)(2,1)S(1)}, bf16[128,128]{1,0:T(8,128)(2,1)}, u32[]{:S(2)}) copy-start(bf16[128,128]{1,0:T(8,128)(2,1)} %param.15) | copy-start | bytes 98308
  9.1 11.5 %copy-start.12 = (bf16[128,128]{1,0:T(8,128)(2,1)S(1)}, bf16[128,128]{1,0:T(8,128)(2,1)}, u32[]{:S(2)}) copy-start(bf16[128,128]{1,0:T(8,128)(2,1)} %param.14) | copy-start | bytes 98308
  9.1 56.2 %copy-start.8 = (f32[128]{0:T(128)S(1)}, f32[128]{0:T(128)}, u32[]{:S(2)}) copy-start(f32[128]{0:T(128)} %param.10) | copy-start | bytes 1540
  9.1 58.0 %all-to-all-start = ((bf16[32,2,128,128]{3,2,1,0:T(8,128)(2,1)}), bf16[32,2,128,128]{3,2,1,0:T(8,128)(2,1)S(1)}, u32[]{:S(2)}, u32[]{:S(2)}) async-start(bf16[32,2,128,128]{3,2,1,0:T(8,128)(2,1)} %bitcast.12), calls=%async_computation | async-start | bytes 4194304 | tf_op jit(solution)/shard_map/spread_vision/all_to_all | solution.py:261
  19.8 45.4 %all-gather.2.cloned.1.call-start = ((), (), s32[]{:S(2)}) async-start(), calls=%async_computation.3 | async-start | bytes 1310720 | tf_op jit(solution)/shard_map/gather_queries/all_gather | solution.py:245
  20.6 22.7 %collective-permute-start.2 = (bf16[1,128,256]{2,1,0:T(8,128)(2,1)S(1)}, bf16[1,128,256]{2,1,0:T(8,128)(2,1)S(1)}, u32[]{:S(2)}, u32[]{:S(2)}) collective-permute-start(bf16[1,128,256]{2,1,0:T(8,128)(2,1)S(1)} %maximum_bitcast_fusion), channel_id=1, source_target_pairs={{0,256},{8,264},{16,272},{24,280},{32,288},{40,296},{48,304},{56,3... | collective-permute-start | bytes 196616 | tf_op jit(solution)/shard_map/gather_projections/ppermute | solution.py:206
  34.1 11.0 %collective-permute-start.1 = (bf16[1,128,256]{2,1,0:T(8,128)(2,1)S(1)}, bf16[1,128,256]{2,1,0:T(8,128)(2,1)S(1)}, u32[]{:S(2)}, u32[]{:S(2)}) collective-permute-start(bf16[1,128,256]{2,1,0:T(8,128)(2,1)S(1)} %maximum_bitcast_fusion), channel_id=1, source_target_pairs={{0,384},{8,392},{16,400},{24,408},{32,416},{40,424},{48,432},{56,4... | collective-permute-start | bytes 196616 | tf_op jit(solution)/shard_map/gather_projections/ppermute | solution.py:206
  36.0 11.0 %collective-permute-start = (bf16[1,128,256]{2,1,0:T(8,128)(2,1)S(1)}, bf16[1,128,256]{2,1,0:T(8,128)(2,1)S(1)}, u32[]{:S(2)}, u32[]{:S(2)}) collective-permute-start(bf16[1,128,256]{2,1,0:T(8,128)(2,1)S(1)} %maximum_bitcast_fusion), channel_id=1, source_target_pairs={{0,128},{8,136},{16,144},{24,152},{32,160},{40,168},{48,176},{56,1... | collective-permute-start | bytes 196616 | tf_op jit(solution)/shard_map/gather_projections/ppermute | solution.py:206
  47.0 10.2 %collective-permute-start.3 = (bf16[4,128,256]{2,1,0:T(8,128)(2,1)S(1)}, bf16[4,128,256]{2,1,0:T(8,128)(2,1)S(1)}, u32[]{:S(2)}, u32[]{:S(2)}) collective-permute-start(bf16[4,128,256]{2,1,0:T(8,128)(2,1)S(1)} %pad_maximum_fusion.refs_0_), channel_id=1, source_target_pairs={{0,32},{8,40},{16,48},{24,56},{32,64},{40,72},{48,80},{56,88},{64,... | collective-permute-start | bytes 786440 | tf_op jit(solution)/shard_map/gather_projections/ppermute | solution.py:206
  51.1 9.6 %collective-permute-start.4 = (bf16[4,128,256]{2,1,0:T(8,128)(2,1)S(1)}, bf16[4,128,256]{2,1,0:T(8,128)(2,1)S(1)}, u32[]{:S(2)}, u32[]{:S(2)}) collective-permute-start(bf16[4,128,256]{2,1,0:T(8,128)(2,1)S(1)} %pad_maximum_fusion.refs_0_), channel_id=1, source_target_pairs={{0,480},{8,488},{16,496},{24,504},{32,0},{40,8},{48,16},{56,24},{6... | collective-permute-start | bytes 786440 | tf_op jit(solution)/shard_map/gather_projections/ppermute | solution.py:206
  57.2 3.5 %copy-start.2 = (bf16[4,128,256]{2,1,0:T(8,128)(2,1)}, bf16[4,128,256]{2,1,0:T(8,128)(2,1)S(1)}, u32[]{:S(2)}) copy-start(bf16[4,128,256]{2,1,0:T(8,128)(2,1)S(1)} %collective-permute-done.3.refs_1_) | copy-start | bytes 786436
  57.9 9.3 %collective-permute-start.5 = (bf16[2,128,256]{2,1,0:T(8,128)(2,1)}, bf16[2,128,256]{2,1,0:T(8,128)(2,1)S(1)}, u32[]{:S(2)}, u32[]{:S(2)}) collective-permute-start(bf16[2,128,256]{2,1,0:T(8,128)(2,1)} %slice.16), channel_id=1, source_target_pairs={{0,32},{8,40},{16,48},{24,56},{32,64},{40,72},{48,80},{56,88},{64,... | collective-permute-start | bytes 393224 | tf_op jit(solution)/shard_map/gather_projections/ppermute | solution.py:206
  60.7 0.7 copy-start.4
  61.5 6.2 %collective-permute-start.6 = (bf16[2,128,256]{2,1,0:T(8,128)(2,1)}, bf16[2,128,256]{2,1,0:T(8,128)(2,1)}, u32[]{:S(2)}, u32[]{:S(2)}) collective-permute-start(bf16[2,128,256]{2,1,0:T(8,128)(2,1)} %slice.17), channel_id=1, source_target_pairs={{0,480},{8,488},{16,496},{24,504},{32,0},{40,8},{48,16},{56,24},{6... | collective-permute-start | bytes 393224 | tf_op jit(solution)/shard_map/gather_projections/ppermute | solution.py:206
  65.3 1.2 copy-start.1
  67.1 20.0 %copy-start.10 = (f32[128]{0:T(128)S(1)}, f32[128]{0:T(128)}, u32[]{:S(2)}) copy-start(f32[128]{0:T(128)} %param.11) | copy-start | bytes 1540
  67.2 63.8 %copy-start.7 = (s32[24]{0:T(128)S(1)}, s32[24]{0:T(128)}, u32[]{:S(2)}) copy-start(s32[24]{0:T(128)} %image_start_ref.3) | copy-start | bytes 292
  67.2 63.8 %copy-start.9 = (s32[128]{0:T(128)S(1)}, s32[128]{0:T(128)}, u32[]{:S(2)}) copy-start(s32[128]{0:T(128)} %slot_image_ref.1) | copy-start | bytes 1540
  67.7 1.0 copy-start.3
  68.6 0.9 copy-start.5
  87.3 17.7 %collective-permute-start.9 = (bf16[1,128,256]{2,1,0:T(8,128)(2,1)S(1)}, bf16[1,128,256]{2,1,0:T(8,128)(2,1)S(1)}, u32[]{:S(2)}, u32[]{:S(2)}) collective-permute-start(bf16[1,128,256]{2,1,0:T(8,128)(2,1)S(1)} %bitcast.13), channel_id=1, source_target_pairs={{0,256},{8,264},{16,272},{24,280},{32,288},{40,296},{48,304},{56,3... | collective-permute-start | bytes 196616 | tf_op jit(solution)/shard_map/gather_keys_values/ppermute | solution.py:206
  95.8 10.1 %collective-permute-start.8 = (bf16[1,128,256]{2,1,0:T(8,128)(2,1)S(1)}, bf16[1,128,256]{2,1,0:T(8,128)(2,1)S(1)}, u32[]{:S(2)}, u32[]{:S(2)}) collective-permute-start(bf16[1,128,256]{2,1,0:T(8,128)(2,1)S(1)} %bitcast.14), channel_id=1, source_target_pairs={{0,384},{8,392},{16,400},{24,408},{32,416},{40,424},{48,432},{56,4... | collective-permute-start | bytes 196616 | tf_op jit(solution)/shard_map/gather_keys_values/ppermute | solution.py:206
  101.4 9.1 %collective-permute-start.7 = (bf16[1,128,256]{2,1,0:T(8,128)(2,1)S(1)}, bf16[1,128,256]{2,1,0:T(8,128)(2,1)S(1)}, u32[]{:S(2)}, u32[]{:S(2)}) collective-permute-start(bf16[1,128,256]{2,1,0:T(8,128)(2,1)S(1)} %bitcast.15), channel_id=1, source_target_pairs={{0,128},{8,136},{16,144},{24,152},{32,160},{40,168},{48,176},{56,1... | collective-permute-start | bytes 196616 | tf_op jit(solution)/shard_map/gather_keys_values/ppermute | solution.py:206
  110.5 9.1 %collective-permute-start.10 = (bf16[4,128,256]{2,1,0:T(8,128)(2,1)S(1)}, bf16[4,128,256]{2,1,0:T(8,128)(2,1)S(1)}, u32[]{:S(2)}, u32[]{:S(2)}) collective-permute-start(bf16[4,128,256]{2,1,0:T(8,128)(2,1)S(1)} %pad_maximum_fusion.1.refs_0_), channel_id=1, source_target_pairs={{0,32},{8,40},{16,48},{24,56},{32,64},{40,72},{48,80},{56,88},{64,... | collective-permute-start | bytes 786440 | tf_op jit(solution)/shard_map/gather_keys_values/ppermute | solution.py:206
  112.4 9.1 %collective-permute-start.11 = (bf16[4,128,256]{2,1,0:T(8,128)(2,1)S(1)}, bf16[4,128,256]{2,1,0:T(8,128)(2,1)S(1)}, u32[]{:S(2)}, u32[]{:S(2)}) collective-permute-start(bf16[4,128,256]{2,1,0:T(8,128)(2,1)S(1)} %pad_maximum_fusion.1.refs_0_), channel_id=1, source_target_pairs={{0,480},{8,488},{16,496},{24,504},{32,0},{40,8},{48,16},{56,24},{6... | collective-permute-start | bytes 786440 | tf_op jit(solution)/shard_map/gather_keys_values/ppermute | solution.py:206
  119.6 6.9 %collective-permute-start.12 = (bf16[2,128,256]{2,1,0:T(8,128)(2,1)S(1)}, bf16[2,128,256]{2,1,0:T(8,128)(2,1)S(1)}, u32[]{:S(2)}, u32[]{:S(2)}) collective-permute-start(bf16[2,128,256]{2,1,0:T(8,128)(2,1)S(1)} %slice.18), channel_id=1, source_target_pairs={{0,32},{8,40},{16,48},{24,56},{32,64},{40,72},{48,80},{56,88},{64,... | collective-permute-start | bytes 393224 | tf_op jit(solution)/shard_map/gather_keys_values/ppermute | solution.py:206
  121.5 9.5 %collective-permute-start.13 = (bf16[2,128,256]{2,1,0:T(8,128)(2,1)S(1)}, bf16[2,128,256]{2,1,0:T(8,128)(2,1)S(1)}, u32[]{:S(2)}, u32[]{:S(2)}) collective-permute-start(bf16[2,128,256]{2,1,0:T(8,128)(2,1)S(1)} %slice.19), channel_id=1, source_target_pairs={{0,480},{8,488},{16,496},{24,504},{32,0},{40,8},{48,16},{56,24},{6... | collective-permute-start | bytes 393224 | tf_op jit(solution)/shard_map/gather_keys_values/ppermute | solution.py:206
  138.3 23.2 %all-to-all-start.2 = ((bf16[4,128,1152]{2,1,0:T(8,128)(2,1)}), bf16[4,128,1152]{2,1,0:T(8,128)(2,1)S(1)}, u32[]{:S(2)}, u32[]{:S(2)}) async-start(bf16[4,128,1152]{2,1,0:T(8,128)(2,1)} %attend.1), calls=%async_computation.2 | async-start | bytes 2359296 | tf_op jit(solution)/shard_map/sum_attention/all_to_all | solution.py:333
Sparse Core Ops, SparseCore 0:
  22.8 31.4 all-gather.1

commit v3 on v2

v3 whole, which is shorter than its diff:
```python
import functools
import math

import jax
import jax.numpy as jnp
from jax import lax
from jax.experimental import pallas as pl
from jax.experimental.pallas import tpu as pltpu
from jax.sharding import PartitionSpec as P

EPS = 1e-05
PLANE = 4
VMEM_LIMIT = 16 * 1024 * 1024
HIDE = -30000.0
STRIDE = 4
SOURCES = ((0, (0, 1, 2, 3)), (-1, (0, 1, 2, 3)), (1, (0, 1, 2, 3)), (2, (0, 1)), (2, (2, 3)))


def source_rank(plane_rank, step, turn):
    return lax.rem(plane_rank + step + STRIDE, STRIDE) + STRIDE * turn


def params(**more):
    return pltpu.CompilerParams(vmem_limit_bytes=VMEM_LIMIT, **more)


def vmem():
    return pl.BlockSpec(memory_space=pltpu.VMEM)


def smem():
    return pl.BlockSpec(memory_space=pltpu.SMEM)


def spread_kernel(x_ref, out_ref):
    members, peers, blocks, _, width = out_ref.shape
    for member in range(members):
        for block in range(blocks):
            first = (block * members + member) * width
            piece = x_ref[:, first : first + width]
            for peer in range(peers):
                out_ref[member, peer, block] = piece


def project_kernel(place_ref, x_ref, *refs):
    weight_refs, out_ref, all_ref = refs[:-2], refs[-2], refs[-1]
    _, depth, width = all_ref.shape
    members, peers, blocks, rows, _ = x_ref.shape
    head_dim = width // 2
    for ref, (step, several) in zip(weight_refs, SOURCES):
        for at, turn in enumerate(several):
            all_ref[source_rank(place_ref[0], step, turn)] = ref[at]
    total = None
    for peer in range(peers):
        for block in range(blocks):
            part = jnp.dot(
                x_ref[:, peer, block].reshape(members * rows, depth),
                all_ref[peer * blocks + block],
                preferred_element_type=jnp.float32,
            )
            total = part if total is None else total + part
    keys = total[:, :head_dim]
    high = keys.astype(jnp.bfloat16)
    low = (keys - high.astype(jnp.float32)).astype(jnp.bfloat16)
    values = total[:, head_dim:].astype(jnp.bfloat16)
    out_ref[...] = jnp.concatenate([high, low, values], axis=1).reshape(out_ref.shape)


def finish_kernel(parts_ref, gain_ref, out_ref):
    raw = jnp.sum(parts_ref[...].astype(jnp.float32), axis=0)
    head_dim = gain_ref.shape[1]
    keys = raw[:, :head_dim] + raw[:, head_dim : 2 * head_dim]
    mean = jnp.mean(keys * keys, axis=-1, keepdims=True)
    keys = keys * lax.rsqrt(mean + EPS) * gain_ref[...]
    out_ref[...] = jnp.concatenate([keys, raw[:, 2 * head_dim :]], axis=1).astype(out_ref.dtype)


def order_of(member):
    return member, member ^ 2, member ^ 1, member ^ 3


def query_kernel(place_ref, q_ref, gain_ref, out_ref):
    heads, all_tokens, head_dim = out_ref.shape
    tokens = all_tokens // PLANE
    for at, member in enumerate(order_of(place_ref[1])):
        rows = pl.ds(pl.multiple_of(member * tokens, tokens), tokens)
        for head in range(heads):
            raw = q_ref[rows, head * head_dim : (head + 1) * head_dim].astype(jnp.float32)
            mean = jnp.mean(raw * raw, axis=-1, keepdims=True)
            out_ref[head, at * tokens : (at + 1) * tokens] = (
                raw * lax.rsqrt(mean + EPS) * gain_ref[...]
            ).astype(out_ref.dtype)


def split_sums(sums, heads):
    column = lax.broadcasted_iota(jnp.int32, sums.shape, 1)
    high = sums.astype(jnp.bfloat16).astype(jnp.float32)
    low = pltpu.roll(sums - high, heads, 1)
    return jnp.where(column < heads, high, jnp.where(column < 2 * heads, low, 0.0))


def join_sums(parts, heads):
    return parts + pltpu.roll(parts, parts.shape[1] - heads, 1)


def attend_kernel(
    image_start_ref,
    slot_image_ref,
    place_ref,
    q_ref,
    *refs,
    scale,
    group,
    slots_here,
):
    kv_refs = refs[:-7]
    out_refs = refs[-7:-4]
    keys_ref, values_ref, late_ref, sums_ref = refs[-4:]
    slots, tile_rows, _ = keys_ref.shape
    ranks = slots // slots_here
    heads, tokens, head_dim = q_ref.shape
    own = tokens // PLANE
    n_images = image_start_ref.shape[0]
    plane_rank = place_ref[0]
    member = place_ref[1]
    first_token = plane_rank * tokens
    limit = first_token + tokens

    lane = lax.broadcasted_iota(jnp.int32, (own, head_dim), 1)
    starts = jnp.full((own, head_dim), ranks * tokens, jnp.int32)
    for image in range(n_images):
        starts = jnp.where(lane == image, image_start_ref[image], starts)
    for at, one in enumerate(order_of(member)):
        position = (
            first_token + one * own + lax.broadcasted_iota(jnp.int32, (own, head_dim), 0)
        )
        late_ref[at * own : (at + 1) * own] = jnp.where(starts > position, 1.0, 0.0).astype(
            jnp.bfloat16
        )

    tile_lane = lax.broadcasted_iota(jnp.int32, (tile_rows, head_dim), 1)
    ones = jnp.ones((tile_rows, head_dim), jnp.bfloat16)

    def put(kept, kv_ref, at, here, image):
        rows = slice(here * tile_rows, (here + 1) * tile_rows)
        mark = jnp.where(tile_lane == image, HIDE, 0.0).astype(jnp.bfloat16)
        keys_ref[kept] = jnp.concatenate([kv_ref[at, rows, :head_dim], mark], axis=1)
        values_ref[kept] = jnp.concatenate([kv_ref[at, rows, head_dim:], ones], axis=1)

    kept = jnp.int32(0)
    for kv_ref, (step, several) in zip(kv_refs, SOURCES):
        for at, turn in enumerate(several):
            rank = source_rank(plane_rank, step, turn)
            for here in range(slots_here):
                image = slot_image_ref[(rank * PLANE + member) * slots_here + here]
                start = image_start_ref[jnp.minimum(image, n_images - 1)]
                seen = jnp.logical_and(image < n_images, start < limit)
                pl.when(seen)(functools.partial(put, kept, kv_ref, at, here, image))
                kept = kept + seen.astype(jnp.int32)
    turns = (kept + group - 1) // group

    def fill(at, _):
        put(at, kv_refs[0], 0, 0, n_images)
        return 0

    lax.fori_loop(kept, turns * group, fill, 0)
    sums_ref[...] = jnp.zeros_like(sums_ref)
    column = lax.broadcasted_iota(jnp.int32, (tokens, head_dim), 1)

    def one_head(head, _, count):
        keys = keys_ref[:count].reshape(count * tile_rows, 2 * head_dim)
        values = values_ref[:count].reshape(count * tile_rows, 2 * head_dim)
        scores = lax.dot_general(
            jnp.concatenate([q_ref[head], late_ref[...]], axis=1),
            keys,
            (((1,), (1,)), ((), ())),
            preferred_element_type=jnp.float32,
        )
        weights = jnp.exp2(scores * scale).astype(jnp.bfloat16)
        total = jnp.dot(weights, values, preferred_element_type=jnp.float32)
        numer = total[:, :head_dim].astype(jnp.bfloat16)
        at = pl.ds(pl.multiple_of(head * head_dim, head_dim), head_dim)
        out_refs[0][:, at] = numer[:own]
        out_refs[1][:, at] = numer[own : 2 * own]
        out_refs[2][:, at] = numer[2 * own :]
        sums_ref[...] = jnp.where(column == head, total[:, head_dim:], sums_ref[...])
        return 0

    for turn in range(1, slots // group + 1):

        @pl.when(turns == turn)
        def _():
            lax.fori_loop(
                0, heads, functools.partial(one_head, count=turn * group), 0, unroll=2
            )

    @pl.when(turns == 0)
    def _():
        for out_ref in out_refs:
            out_ref[...] = jnp.zeros_like(out_ref)

    sums = split_sums(sums_ref[...], heads).astype(jnp.bfloat16)
    out_refs[0][:, heads * head_dim :] = sums[:own]
    out_refs[1][:, heads * head_dim :] = sums[own : 2 * own]
    out_refs[2][:, heads * head_dim :] = sums[2 * own :]


def add_kernel(kept_ref, came_ref, out_ref, *, heads):
    own, width = kept_ref.shape
    cut = width - 128
    for first in range(0, cut, 256):
        columns = slice(first, min(first + 256, cut))
        out_ref[:, columns] = (
            kept_ref[:, columns].astype(jnp.float32)
            + came_ref[own:, columns].astype(jnp.float32)
        ).astype(out_ref.dtype)
    sums = kept_ref[:, cut:].astype(jnp.float32) + came_ref[own:, cut:].astype(jnp.float32)
    out_ref[:, cut:] = split_sums(join_sums(sums, heads), heads).astype(out_ref.dtype)


def combine_kernel(image_start_ref, place_ref, gate_ref, kept_ref, core_ref, chip_ref, out_ref):
    own, width = kept_ref.shape
    out_width = out_ref.shape[1]
    head_dim = width - out_width
    heads = out_width // head_dim
    first = (place_ref[0] * PLANE + place_ref[1]) * own
    position = first + lax.broadcasted_iota(jnp.int32, (own, 1), 0)
    seen = position >= image_start_ref[0]
    factor = jnp.tanh(gate_ref[...])

    def total(columns):
        return (
            kept_ref[:, columns].astype(jnp.float32)
            + core_ref[:own, columns].astype(jnp.float32)
            + chip_ref[:, columns].astype(jnp.float32)
        )

    sums = join_sums(total(slice(out_width, width)), heads)
    for head in range(heads):
        columns = slice(head * head_dim, (head + 1) * head_dim)
        safe = jnp.where(seen, sums[:, head : head + 1], 1.0)
        out_ref[:, columns] = jnp.where(seen, total(columns) * (factor / safe), 0.0).astype(
            out_ref.dtype
        )


def gather_along_z(block):
    ctx_size = lax.axis_size("ctx")
    ranks = ctx_size // PLANE

    def shift(value, distance):
        moved = distance * PLANE
        return lax.ppermute(
            value, "ctx", [(i, (i + moved) % ctx_size) for i in range(ctx_size)]
        )

    groups = [
        [rank * PLANE + member for rank in range(first, ranks, STRIDE)]
        for member in range(PLANE)
        for first in range(STRIDE)
    ]
    own = lax.all_gather(block, "ctx", axis_index_groups=groups)
    half = own.shape[0] // 2
    return own, shift(own, 1), shift(own, -1), shift(own[:half], 2), shift(own[half:], -2)


def other_member(value, mask):
    ctx_size = lax.axis_size("ctx")
    return lax.ppermute(value, "ctx", [(i, i ^ mask) for i in range(ctx_size)])


def local(
    queries,
    q_gain,
    k_gain,
    attn_gate,
    vision,
    key_projection_matrix,
    value_projection_matrix,
    image_start,
    slot_image,
):
    ctx_size = lax.axis_size("ctx")
    head_size = lax.axis_size("head")
    ranks = ctx_size // PLANE
    own_index = lax.axis_index("ctx")
    plane_rank = own_index // PLANE
    member = own_index % PLANE
    place = jnp.stack([plane_rank, member]).astype(jnp.int32)
    head_dim = q_gain.shape[0]
    tokens, q_cols = queries.shape
    heads = q_cols // head_dim
    rows, features = vision.shape
    piece_rows, kv_cols = key_projection_matrix.shape
    in_plane = [[rank * PLANE + m for m in range(PLANE)] for rank in range(ranks)]
    whole_plane = [
        [rank * PLANE * head_size + i for i in range(PLANE * head_size)] for rank in range(ranks)
    ]

    with jax.named_scope("gather_queries"):
        all_queries = lax.all_gather(
            queries, "ctx", axis_index_groups=in_plane, axis=0, tiled=True
        )

    with jax.named_scope("spread_vision"):
        blocks = features // (piece_rows * PLANE)
        mine = pl.pallas_call(
            spread_kernel,
            out_shape=jax.ShapeDtypeStruct(
                (PLANE, head_size, blocks, rows, piece_rows), jnp.bfloat16
            ),
            in_specs=[vmem()],
            out_specs=vmem(),
            compiler_params=params(),
        )(vision)
        mine = mine.reshape(PLANE * head_size, blocks, rows, piece_rows)
        spread = lax.all_to_all(mine, ("ctx", "head"), 0, 0, axis_index_groups=whole_plane)
        spread = spread.reshape(PLANE, head_size, blocks, rows, piece_rows)

    with jax.named_scope("gather_projections"):
        weights = gather_along_z(
            jnp.concatenate([key_projection_matrix, value_projection_matrix], axis=1)
        )

    with jax.named_scope("norm_queries"):
        normed = pl.pallas_call(
            query_kernel,
            out_shape=jax.ShapeDtypeStruct((heads, PLANE * tokens, head_dim), jnp.bfloat16),
            in_specs=[smem(), vmem(), vmem()],
            out_specs=vmem(),
            compiler_params=params(),
        )(place, all_queries, q_gain.reshape(1, head_dim))
        spread, normed = lax.optimization_barrier((spread, normed))

    with jax.named_scope("project"):
        partial = pl.pallas_call(
            project_kernel,
            out_shape=jax.ShapeDtypeStruct((PLANE, rows, 3 * kv_cols), jnp.bfloat16),
            in_specs=[smem()] + [vmem()] * (1 + len(weights)),
            out_specs=vmem(),
            scratch_shapes=[pltpu.VMEM((ranks, piece_rows, 2 * kv_cols), jnp.bfloat16)],
            compiler_params=params(),
        )(place, spread, *weights)

    with jax.named_scope("sum_projections"):
        partial = lax.all_to_all(partial, "ctx", 0, 0, axis_index_groups=in_plane)
        own_kv = pl.pallas_call(
            finish_kernel,
            out_shape=jax.ShapeDtypeStruct((rows, 2 * kv_cols), jnp.bfloat16),
            in_specs=[vmem(), vmem()],
            out_specs=vmem(),
            compiler_params=params(),
        )(partial, k_gain.reshape(1, head_dim))

    with jax.named_scope("gather_keys_values"):
        all_kv = gather_along_z(own_kv)

    with jax.named_scope("attend"):
        slots_here = slot_image.shape[0] // ctx_size
        tile_rows = rows // slots_here
        slots = ranks * slots_here
        width = q_cols + head_dim
        shapes = [(tokens, width), (tokens, width), (2 * tokens, width)]
        kept, to_chip, to_core = pl.pallas_call(
            functools.partial(
                attend_kernel,
                scale=head_dim ** (-0.5) * math.log2(math.e),
                group=math.gcd(slots, 4),
                slots_here=slots_here,
            ),
            out_shape=[jax.ShapeDtypeStruct(shape, jnp.bfloat16) for shape in shapes],
            in_specs=[smem()] * 3 + [vmem()] * (1 + len(all_kv)),
            out_specs=[vmem()] * 3,
            scratch_shapes=[
                pltpu.VMEM((slots, tile_rows, 2 * head_dim), jnp.bfloat16),
                pltpu.VMEM((slots, tile_rows, 2 * head_dim), jnp.bfloat16),
                pltpu.VMEM((PLANE * tokens, head_dim), jnp.bfloat16),
                pltpu.VMEM((PLANE * tokens, head_dim), jnp.float32),
            ],
            compiler_params=params(),
        )(image_start, slot_image, place, normed, *all_kv)

    with jax.named_scope("sum_attention"):
        from_core = other_member(to_core, 1)
        to_chip = pl.pallas_call(
            functools.partial(add_kernel, heads=heads),
            out_shape=jax.ShapeDtypeStruct((tokens, width), jnp.bfloat16),
            in_specs=[vmem(), vmem()],
            out_specs=vmem(),
            compiler_params=params(),
        )(to_chip, from_core)
        from_chip = other_member(to_chip, 2)
        return pl.pallas_call(
            combine_kernel,
            out_shape=jax.ShapeDtypeStruct((tokens, q_cols), jnp.bfloat16),
            in_specs=[smem(), smem()] + [vmem()] * 4,
            out_specs=vmem(),
            compiler_params=params(),
        )(image_start, place, attn_gate.reshape(1, 1), kept, from_core, from_chip)


def solution(mesh):
    in_specs = (
        P("ctx", "head"),
        P(),
        P(),
        P(),
        P("ctx", "head"),
        P("ctx", "head"),
        P("ctx", "head"),
        P(),
        P(),
    )
    out_specs = P("ctx", "head")
    return jax.shard_map(local, mesh=mesh, in_specs=in_specs, out_specs=out_specs, check_vma=False)
```

time: 173 us -> 150 us (0.87); the launches traced: 170 us -> 149 us
  blocking collectives: 15.3 us -> 56.4 us
  starting transfers between devices: 85.1 us -> 46.3 us
  waiting for transfers between devices: 35.9 us -> 17.3 us
  local copies, waits for them, and re-layouts: 6.91 us -> 4.25 us
    ppermute x14 -> x8, starting transfers between devices: 67.7 us -> 28 us  [shift(): lax.ppermute(value, 'ctx', [(i, (i + moved) % ctx_size) for i in range(ct...]
    all_gather x0 -> x2, blocking collectives: none -> 38.3 us  [gather_along_z(): own = lax.all_gather(block, 'ctx', axis_index_groups=groups)]
    all_to_all x1 -> x0, waiting for transfers between devices: 15.9 us -> none  [local(): packed = lax.all_to_all(packed, 'ctx', 0, 0, axis_index_groups=in_plane)]
    ppermute x14 -> x8, waiting for transfers between devices: 19.3 us -> 6.14 us  [shift(): lax.ppermute(value, 'ctx', [(i, (i + moved) % ctx_size) for i in range(ct...]
    ppermute x0 -> x2, waiting for transfers between devices: none -> 10.5 us  [other_member(): return lax.ppermute(value, 'ctx', [(i, i ^ mask) for i in range(ctx_size)])]
    ppermute x0 -> x2, starting transfers between devices: none -> 7.5 us  [other_member(): return lax.ppermute(value, 'ctx', [(i, i ^ mask) for i in range(ctx_size)])]
    all_to_all x1 -> x0, starting transfers between devices: 6.69 us -> none  [local(): packed = lax.all_to_all(packed, 'ctx', 0, 0, axis_index_groups=in_plane)]
    all_to_all x1, blocking collectives: 15.3 us -> 18.1 us  [local(): partial = lax.all_to_all(partial, 'ctx', 0, 0, axis_index_groups=in_plane)]
  transfers between devices with their start and end apart: 17 -> 12, of which waited for: 10 -> 5; matrix products, arithmetic and copies ran while one was open for 1% -> 1% of each run, Pallas kernels for 0% -> 1%
where the time goes in v3:
time: 150 us; the launch traced here: 149 us
  blocking collectives  56.4 us (38%)
  starting transfers between devices  46.3 us (31%)
  waiting for transfers between devices  17.3 us (12%)
  between operations  14.3 us (10%)
  Pallas kernels  10.9 us (7%)
  local copies, waits for them, and re-layouts  4.25 us (3%)
    all_gather x2, blocking collectives, gather_along_z(): own = lax.all_gather(block, 'ctx', axis_index_groups=groups)  38.3 us
    ppermute x8, starting transfers between devices, shift(): lax.ppermute(value, 'ctx', [(i, (i + moved) % ctx_size) for i in range(ct...  28 us
    all_to_all x1, blocking collectives, local(): partial = lax.all_to_all(partial, 'ctx', 0, 0, axis_index_groups=in_plane)  18.1 us
    all_to_all x1, starting transfers between devices, local(): lax.all_to_all(mine, ('ctx', 'head'), 0, 0, axis_index_groups=whole_plane)  10.7 us
    ppermute x2, waiting for transfers between devices, other_member(): return lax.ppermute(value, 'ctx', [(i, i ^ mask) for i in range(ctx_size)])  10.5 us
    ppermute x2, starting transfers between devices, other_member(): return lax.ppermute(value, 'ctx', [(i, i ^ mask) for i in range(ctx_size)])  7.5 us
    ppermute x8, waiting for transfers between devices, shift(): lax.ppermute(value, 'ctx', [(i, (i + moved) % ctx_size) for i in range(ct...  6.14 us
    pallas_call x1, Pallas kernels, local(): pl.pallas_call(functools.partial(attend_kernel, scale=head_dim ** (-0.5)...  4.88 us
  transfers between devices with their start and end apart: 12, of which 5 were waited for; matrix products, arithmetic and copies ran while one was open for 1% of the time, Pallas kernels for 1%

profile of v3, /device:TPU:1, one launch (start us, length us, event | category | flops | bytes accessed | tf_op | source)
XLA Modules:
  0.0 149.5 jit_solution(15003724376551420683)
XLA Ops:
  6.5 0.9 copy-done.2
  7.5 0.3 spread_vision.1
  7.8 0.0 copy-start
  7.8 1.3 copy-done
  9.1 10.7 %all-to-all-start = ((bf16[32,2,128,128]{3,2,1,0:T(8,128)(2,1)}), bf16[32,2,128,128]{3,2,1,0:T(8,128)(2,1)S(1)}, u32[]{:S(2)}, u32[]{:S(2)}) async-start(bf16[32,2,128,128]{3,2,1,0:T(8,128)(2,1)} %bitcast.15), calls=%async_computation | async-start | bytes 4194304 | tf_op jit(solution)/shard_map/spread_vision/all_to_all | solution.py:317
  19.8 0.0 all-gather.4.cloned.1.call-start
  19.9 0.7 all-gather.4.cloned.1.call-update
  20.6 0.0 copy-done.7
  20.6 0.0 copy-done.8
  20.6 22.4 %all-gather = bf16[512,256]{1,0:T(8,128)(2,1)S(1)} all-gather(bf16[128,256]{1,0:T(8,128)(2,1)S(1)} %pad_maximum_fusion), channel_id=2, replica_groups={{0,128,256,384},{32,160,288,416},{64,192,320,448},{96,224,352,480},{8,1..., dimensions={0}, use_global_device_ids=true | all-gather | bytes 327680 | tf_op jit(solution)/shard_map/gather_projections/all_gather | solution.py:262
  43.0 2.9 %collective-permute-start = (bf16[4,128,256]{2,1,0:T(8,128)(2,1)S(1)}, bf16[4,128,256]{2,1,0:T(8,128)(2,1)}, u32[]{:S(2)}, u32[]{:S(2)}) collective-permute-start(bf16[4,128,256]{2,1,0:T(8,128)(2,1)S(1)} %bitcast.19), channel_id=1, source_target_pairs={{0,32},{8,40},{16,48},{24,56},{32,64},{40,72},{48,80},{56,88},{64,... | collective-permute-start | bytes 786440 | tf_op jit(solution)/shard_map/gather_projections/ppermute | solution.py:253
  45.9 3.6 %collective-permute-start.1 = (bf16[4,128,256]{2,1,0:T(8,128)(2,1)S(1)}, bf16[4,128,256]{2,1,0:T(8,128)(2,1)}, u32[]{:S(2)}, u32[]{:S(2)}) collective-permute-start(bf16[4,128,256]{2,1,0:T(8,128)(2,1)S(1)} %bitcast.20), channel_id=1, source_target_pairs={{0,480},{8,488},{16,496},{24,504},{32,0},{40,8},{48,16},{56,24},{6... | collective-permute-start | bytes 786440 | tf_op jit(solution)/shard_map/gather_projections/ppermute | solution.py:253
  49.5 0.7 fusion.1
  50.2 2.3 %collective-permute-start.2 = (bf16[2,128,256]{2,1,0:T(8,128)(2,1)}, bf16[2,128,256]{2,1,0:T(8,128)(2,1)S(1)}, u32[]{:S(2)}, u32[]{:S(2)}) collective-permute-start(bf16[2,128,256]{2,1,0:T(8,128)(2,1)} %bitcast.7), channel_id=1, source_target_pairs={{0,64},{8,72},{16,80},{24,88},{32,96},{40,104},{48,112},{56,120},{... | collective-permute-start | bytes 393224 | tf_op jit(solution)/shard_map/gather_projections/ppermute | solution.py:253
  52.5 5.1 %collective-permute-start.3 = (bf16[2,128,256]{2,1,0:T(8,128)(2,1)}, bf16[2,128,256]{2,1,0:T(8,128)(2,1)}, u32[]{:S(2)}, u32[]{:S(2)}) collective-permute-start(bf16[2,128,256]{2,1,0:T(8,128)(2,1)} %bitcast.8), channel_id=1, source_target_pairs={{0,448},{8,456},{16,464},{24,472},{32,480},{40,488},{48,496},{56,5... | collective-permute-start | bytes 393224 | tf_op jit(solution)/shard_map/gather_projections/ppermute | solution.py:253
  57.6 0.1 pad_add_fusion.place_ref
  57.7 0.0 copy-done.6
  57.7 1.2 copy-done.1
  58.9 1.2 norm_queries.1.q_ref
  60.1 0.0 all-to-all-done
  60.1 0.0 copy-start.5
  60.1 0.0 copy-start.3
  60.1 0.0 copy-start.4
  60.1 0.0 collective-permute-done.2.refs_3_
  60.2 0.6 collective-permute-done.3.refs_4_
  60.8 0.0 collective-permute-done.refs_1_
  60.8 0.0 collective-permute-done.1.refs_2_
  60.8 2.4 %project.1 = bf16[4,128,384]{2,1,0:T(8,128)(2,1)S(1)} custom-call(s32[2]{0:T(128)S(1)} %pad_add_fusion.place_ref, bf16[4,8,2,128,128]{4,3,2,1,0:T(8,128)(2,1)S(1)} %bitcast.14, bf16[4,128,256]{2,1,0:T(8,128)(2,1)S(1)} %bitcast.21, bf16[4,128,256]{2,1,0:T(8,128)(2,1)} %collective-permute-done.refs_1_, bf16[4,128,256]{2,1,0:T(8,128)(2,1)} %collective-permute-done.1.refs_2_, ...), custom_call_target="tpu_custom_call" | custom-call | tf_op jit(solution)/shard_map/project/pallas_call | solution.py:336
  63.2 18.1 %all_to_all.10.parts_ref = bf16[4,128,384]{2,1,0:T(8,128)(2,1)S(1)} all-to-all(bf16[4,128,384]{2,1,0:T(8,128)(2,1)S(1)} %project.1), channel_id=1, replica_groups={{0,8,16,24},{32,40,48,56},{64,72,80,88},{96,104,112,120},{128,136,144,1..., dimensions={0} | all-to-all | bytes 786432 | tf_op jit(solution)/shard_map/sum_projections/all_to_all | solution.py:346
  81.2 0.0 copy-done.5
  81.2 0.1 sum_projections.1
  81.4 15.9 %all-gather.1 = bf16[512,256]{1,0:T(8,128)(2,1)S(1)} all-gather(bf16[128,256]{1,0:T(8,128)(2,1)S(1)} %sum_projections.1), channel_id=3, replica_groups={{0,128,256,384},{32,160,288,416},{64,192,320,448},{96,224,352,480},{8,1..., dimensions={0}, use_global_device_ids=true | all-gather | bytes 327680 | tf_op jit(solution)/shard_map/gather_keys_values/all_gather | solution.py:262
  97.3 1.9 %collective-permute-start.4 = (bf16[4,128,256]{2,1,0:T(8,128)(2,1)S(1)}, bf16[4,128,256]{2,1,0:T(8,128)(2,1)S(1)}, u32[]{:S(2)}, u32[]{:S(2)}) collective-permute-start(bf16[4,128,256]{2,1,0:T(8,128)(2,1)S(1)} %bitcast.16), channel_id=1, source_target_pairs={{0,32},{8,40},{16,48},{24,56},{32,64},{40,72},{48,80},{56,88},{64,... | collective-permute-start | bytes 786440 | tf_op jit(solution)/shard_map/gather_keys_values/ppermute | solution.py:253
  99.2 4.6 %collective-permute-start.5 = (bf16[4,128,256]{2,1,0:T(8,128)(2,1)S(1)}, bf16[4,128,256]{2,1,0:T(8,128)(2,1)S(1)}, u32[]{:S(2)}, u32[]{:S(2)}) collective-permute-start(bf16[4,128,256]{2,1,0:T(8,128)(2,1)S(1)} %bitcast.17), channel_id=1, source_target_pairs={{0,480},{8,488},{16,496},{24,504},{32,0},{40,8},{48,16},{56,24},{6... | collective-permute-start | bytes 786440 | tf_op jit(solution)/shard_map/gather_keys_values/ppermute | solution.py:253
  103.8 3.5 %collective-permute-start.6 = (bf16[2,128,256]{2,1,0:T(8,128)(2,1)S(1)}, bf16[2,128,256]{2,1,0:T(8,128)(2,1)S(1)}, u32[]{:S(2)}, u32[]{:S(2)}) collective-permute-start(bf16[2,128,256]{2,1,0:T(8,128)(2,1)S(1)} %bitcast.25), channel_id=1, source_target_pairs={{0,64},{8,72},{16,80},{24,88},{32,96},{40,104},{48,112},{56,120},{... | collective-permute-start | bytes 393224 | tf_op jit(solution)/shard_map/gather_keys_values/ppermute | solution.py:253
  107.3 4.2 %collective-permute-start.7 = (bf16[2,128,256]{2,1,0:T(8,128)(2,1)S(1)}, bf16[2,128,256]{2,1,0:T(8,128)(2,1)S(1)}, u32[]{:S(2)}, u32[]{:S(2)}) collective-permute-start(bf16[2,128,256]{2,1,0:T(8,128)(2,1)S(1)} %bitcast.24), channel_id=1, source_target_pairs={{0,448},{8,456},{16,464},{24,472},{32,480},{40,488},{48,496},{56,5... | collective-permute-start | bytes 393224 | tf_op jit(solution)/shard_map/gather_keys_values/ppermute | solution.py:253
  111.5 2.5 %collective-permute-done.6.refs_3_ = bf16[2,128,256]{2,1,0:T(8,128)(2,1)S(1)} collective-permute-done((bf16[2,128,256]{2,1,0:T(8,128)(2,1)S(1)}, bf16[2,128,256]{2,1,0:T(8,128)(2,1)S(1)}, u32[]{:S(2)}, u32[]{:S(2)}) %collective-permute-start.6) | collective-permute-done | bytes 131104 | tf_op jit(solution)/shard_map/gather_keys_values/ppermute | solution.py:253
  114.0 2.9 %collective-permute-done.7.refs_4_ = bf16[2,128,256]{2,1,0:T(8,128)(2,1)S(1)} collective-permute-done((bf16[2,128,256]{2,1,0:T(8,128)(2,1)S(1)}, bf16[2,128,256]{2,1,0:T(8,128)(2,1)S(1)}, u32[]{:S(2)}, u32[]{:S(2)}) %collective-permute-start.7) | collective-permute-done | bytes 131104 | tf_op jit(solution)/shard_map/gather_keys_values/ppermute | solution.py:253
  117.0 0.0 collective-permute-done.4.refs_1_
  117.0 0.0 collective-permute-done.5.refs_2_
  117.0 0.0 copy-done.3
  117.0 4.9 %attend.1 = (bf16[128,1152]{1,0:T(8,128)(2,1)S(1)}, bf16[128,1152]{1,0:T(8,128)(2,1)S(1)}, bf16[256,1152]{1,0:T(8,128)(2,1)S(1)}) custom-call(s32[24]{0:T(128)S(1)} %copy-done.3, s32[128]{0:T(128)S(1)} %copy-done.4, s32[2]{0:T(128)S(1)} %pad_add_fusion.place_ref, bf16[8,512,128]{2,1,0:T(8,128)(2,1)S(1)} %norm_queries.1.q_ref, ...), custom_call_target="tpu_custom_call" | custom-call | tf_op jit(solution)/shard_map/attend/pallas_call | solution.py:364
  121.9 5.4 %collective-permute-start.8 = (bf16[256,1152]{1,0:T(8,128)(2,1)S(1)}, bf16[256,1152]{1,0:T(8,128)(2,1)S(1)}, u32[]{:S(2)}, u32[]{:S(2)}) collective-permute-start(bf16[256,1152]{1,0:T(8,128)(2,1)S(1)} %get-tuple-element.13), channel_id=1, source_target_pairs={{0,8},{8,0},{16,24},{24,16},{32,40},{40,32},{48,56},{56,48},{64,72... | collective-permute-start | bytes 1769480 | tf_op jit(solution)/shard_map/sum_attention/ppermute | solution.py:269
  127.3 1.6 %collective-permute-done.8.came_ref.core_ref = bf16[256,1152]{1,0:T(8,128)(2,1)S(1)} collective-permute-done((bf16[256,1152]{1,0:T(8,128)(2,1)S(1)}, bf16[256,1152]{1,0:T(8,128)(2,1)S(1)}, u32[]{:S(2)}, u32[]{:S(2)}) %collective-permute-start.8) | collective-permute-done | bytes 589856 | tf_op jit(solution)/shard_map/sum_attention/ppermute | solution.py:269
  128.9 0.2 sum_attention.2
  129.2 2.1 %collective-permute-start.9 = (bf16[128,1152]{1,0:T(8,128)(2,1)S(1)}, bf16[128,1152]{1,0:T(8,128)(2,1)S(1)}, u32[]{:S(2)}, u32[]{:S(2)}) collective-permute-start(bf16[128,1152]{1,0:T(8,128)(2,1)S(1)} %sum_attention.2), channel_id=1, source_target_pairs={{0,16},{8,24},{16,0},{24,8},{32,48},{40,56},{48,32},{56,40},{64,80... | collective-permute-start | bytes 884744 | tf_op jit(solution)/shard_map/sum_attention/ppermute | solution.py:269
  131.9 8.9 %collective-permute-done.9.chip_ref = bf16[128,1152]{1,0:T(8,128)(2,1)S(1)} collective-permute-done((bf16[128,1152]{1,0:T(8,128)(2,1)S(1)}, bf16[128,1152]{1,0:T(8,128)(2,1)S(1)}, u32[]{:S(2)}, u32[]{:S(2)}) %collective-permute-start.9) | collective-permute-done | bytes 294944 | tf_op jit(solution)/shard_map/sum_attention/ppermute | solution.py:269
  140.8 1.9 %sum_attention.3 = bf16[128,1024]{1,0:T(8,128)(2,1)} custom-call(s32[24]{0:T(128)S(1)} %copy-done.3, s32[2]{0:T(128)S(1)} %pad_add_fusion.place_ref, f32[1,1]{1,0:T(1,128)} %bitcast.13.gate_ref, bf16[128,1152]{1,0:T(8,128)(2,1)S(1)} %get-tuple-element.12.kept_ref, bf16[256,1152]{1,0:T(8,128)(2,1)S(1)} %collective-permute-done.8.came_ref.core_ref, ...), custom_call_target="tpu_custom_call" | custom-call | tf_op jit(solution)/shard_map/sum_attention/pallas_call | solution.py:393
  (9 shorter events, 0.0 us)
Async XLA Ops:
  6.5 0.9 copy-start.2
  7.8 1.3 copy-start
  9.1 11.5 %copy-start.7 = (bf16[128,128]{1,0:T(8,128)(2,1)S(1)}, bf16[128,128]{1,0:T(8,128)(2,1)}, u32[]{:S(2)}) copy-start(bf16[128,128]{1,0:T(8,128)(2,1)} %param.15) | copy-start | bytes 98308
  9.1 11.5 %copy-start.8 = (bf16[128,128]{1,0:T(8,128)(2,1)S(1)}, bf16[128,128]{1,0:T(8,128)(2,1)}, u32[]{:S(2)}) copy-start(bf16[128,128]{1,0:T(8,128)(2,1)} %param.14) | copy-start | bytes 98308
  9.1 48.6 %copy-start.6 = (f32[128]{0:T(128)S(1)}, f32[128]{0:T(128)}, u32[]{:S(2)}) copy-start(f32[128]{0:T(128)} %param.10) | copy-start | bytes 1540
  9.1 51.0 %all-to-all-start = ((bf16[32,2,128,128]{3,2,1,0:T(8,128)(2,1)}), bf16[32,2,128,128]{3,2,1,0:T(8,128)(2,1)S(1)}, u32[]{:S(2)}, u32[]{:S(2)}) async-start(bf16[32,2,128,128]{3,2,1,0:T(8,128)(2,1)} %bitcast.15), calls=%async_computation | async-start | bytes 4194304 | tf_op jit(solution)/shard_map/spread_vision/all_to_all | solution.py:317
  19.8 37.9 %all-gather.4.cloned.1.call-start = ((), (), s32[]{:S(2)}) async-start(), calls=%async_computation.2 | async-start | bytes 1310720 | tf_op jit(solution)/shard_map/gather_queries/all_gather | solution.py:301
  43.0 17.8 %collective-permute-start = (bf16[4,128,256]{2,1,0:T(8,128)(2,1)S(1)}, bf16[4,128,256]{2,1,0:T(8,128)(2,1)}, u32[]{:S(2)}, u32[]{:S(2)}) collective-permute-start(bf16[4,128,256]{2,1,0:T(8,128)(2,1)S(1)} %bitcast.19), channel_id=1, source_target_pairs={{0,32},{8,40},{16,48},{24,56},{32,64},{40,72},{48,80},{56,88},{64,... | collective-permute-start | bytes 786440 | tf_op jit(solution)/shard_map/gather_projections/ppermute | solution.py:253
  45.9 14.9 %collective-permute-start.1 = (bf16[4,128,256]{2,1,0:T(8,128)(2,1)S(1)}, bf16[4,128,256]{2,1,0:T(8,128)(2,1)}, u32[]{:S(2)}, u32[]{:S(2)}) collective-permute-start(bf16[4,128,256]{2,1,0:T(8,128)(2,1)S(1)} %bitcast.20), channel_id=1, source_target_pairs={{0,480},{8,488},{16,496},{24,504},{32,0},{40,8},{48,16},{56,24},{6... | collective-permute-start | bytes 786440 | tf_op jit(solution)/shard_map/gather_projections/ppermute | solution.py:253
  50.2 10.0 %collective-permute-start.2 = (bf16[2,128,256]{2,1,0:T(8,128)(2,1)}, bf16[2,128,256]{2,1,0:T(8,128)(2,1)S(1)}, u32[]{:S(2)}, u32[]{:S(2)}) collective-permute-start(bf16[2,128,256]{2,1,0:T(8,128)(2,1)} %bitcast.7), channel_id=1, source_target_pairs={{0,64},{8,72},{16,80},{24,88},{32,96},{40,104},{48,112},{56,120},{... | collective-permute-start | bytes 393224 | tf_op jit(solution)/shard_map/gather_projections/ppermute | solution.py:253
  52.5 8.3 %collective-permute-start.3 = (bf16[2,128,256]{2,1,0:T(8,128)(2,1)}, bf16[2,128,256]{2,1,0:T(8,128)(2,1)}, u32[]{:S(2)}, u32[]{:S(2)}) collective-permute-start(bf16[2,128,256]{2,1,0:T(8,128)(2,1)} %bitcast.8), channel_id=1, source_target_pairs={{0,448},{8,456},{16,464},{24,472},{32,480},{40,488},{48,496},{56,5... | collective-permute-start | bytes 393224 | tf_op jit(solution)/shard_map/gather_projections/ppermute | solution.py:253
  57.7 1.2 copy-start.1
  60.1 21.1 %copy-start.5 = (f32[128]{0:T(128)S(1)}, f32[128]{0:T(128)}, u32[]{:S(2)}) copy-start(f32[128]{0:T(128)} %param.11) | copy-start | bytes 1540
  60.1 56.9 %copy-start.3 = (s32[24]{0:T(128)S(1)}, s32[24]{0:T(128)}, u32[]{:S(2)}) copy-start(s32[24]{0:T(128)} %image_start_ref.3) | copy-start | bytes 292
  60.1 56.9 %copy-start.4 = (s32[128]{0:T(128)S(1)}, s32[128]{0:T(128)}, u32[]{:S(2)}) copy-start(s32[128]{0:T(128)} %slot_image_ref.1) | copy-start | bytes 1540
  97.3 19.7 %collective-permute-start.4 = (bf16[4,128,256]{2,1,0:T(8,128)(2,1)S(1)}, bf16[4,128,256]{2,1,0:T(8,128)(2,1)S(1)}, u32[]{:S(2)}, u32[]{:S(2)}) collective-permute-start(bf16[4,128,256]{2,1,0:T(8,128)(2,1)S(1)} %bitcast.16), channel_id=1, source_target_pairs={{0,32},{8,40},{16,48},{24,56},{32,64},{40,72},{48,80},{56,88},{64,... | collective-permute-start | bytes 786440 | tf_op jit(solution)/shard_map/gather_keys_values/ppermute | solution.py:253
  99.2 17.8 %collective-permute-start.5 = (bf16[4,128,256]{2,1,0:T(8,128)(2,1)S(1)}, bf16[4,128,256]{2,1,0:T(8,128)(2,1)S(1)}, u32[]{:S(2)}, u32[]{:S(2)}) collective-permute-start(bf16[4,128,256]{2,1,0:T(8,128)(2,1)S(1)} %bitcast.17), channel_id=1, source_target_pairs={{0,480},{8,488},{16,496},{24,504},{32,0},{40,8},{48,16},{56,24},{6... | collective-permute-start | bytes 786440 | tf_op jit(solution)/shard_map/gather_keys_values/ppermute | solution.py:253
  103.8 10.2 %collective-permute-start.6 = (bf16[2,128,256]{2,1,0:T(8,128)(2,1)S(1)}, bf16[2,128,256]{2,1,0:T(8,128)(2,1)S(1)}, u32[]{:S(2)}, u32[]{:S(2)}) collective-permute-start(bf16[2,128,256]{2,1,0:T(8,128)(2,1)S(1)} %bitcast.25), channel_id=1, source_target_pairs={{0,64},{8,72},{16,80},{24,88},{32,96},{40,104},{48,112},{56,120},{... | collective-permute-start | bytes 393224 | tf_op jit(solution)/shard_map/gather_keys_values/ppermute | solution.py:253
  107.3 9.7 %collective-permute-start.7 = (bf16[2,128,256]{2,1,0:T(8,128)(2,1)S(1)}, bf16[2,128,256]{2,1,0:T(8,128)(2,1)S(1)}, u32[]{:S(2)}, u32[]{:S(2)}) collective-permute-start(bf16[2,128,256]{2,1,0:T(8,128)(2,1)S(1)} %bitcast.24), channel_id=1, source_target_pairs={{0,448},{8,456},{16,464},{24,472},{32,480},{40,488},{48,496},{56,5... | collective-permute-start | bytes 393224 | tf_op jit(solution)/shard_map/gather_keys_values/ppermute | solution.py:253
  121.9 7.0 %collective-permute-start.8 = (bf16[256,1152]{1,0:T(8,128)(2,1)S(1)}, bf16[256,1152]{1,0:T(8,128)(2,1)S(1)}, u32[]{:S(2)}, u32[]{:S(2)}) collective-permute-start(bf16[256,1152]{1,0:T(8,128)(2,1)S(1)} %get-tuple-element.13), channel_id=1, source_target_pairs={{0,8},{8,0},{16,24},{24,16},{32,40},{40,32},{48,56},{56,48},{64,72... | collective-permute-start | bytes 1769480 | tf_op jit(solution)/shard_map/sum_attention/ppermute | solution.py:269
  129.2 11.6 %collective-permute-start.9 = (bf16[128,1152]{1,0:T(8,128)(2,1)S(1)}, bf16[128,1152]{1,0:T(8,128)(2,1)S(1)}, u32[]{:S(2)}, u32[]{:S(2)}) collective-permute-start(bf16[128,1152]{1,0:T(8,128)(2,1)S(1)} %sum_attention.2), channel_id=1, source_target_pairs={{0,16},{8,24},{16,0},{24,8},{32,48},{40,56},{48,32},{56,40},{64,80... | collective-permute-start | bytes 884744 | tf_op jit(solution)/shard_map/sum_attention/ppermute | solution.py:269
Sparse Core Ops, SparseCore 0:
  22.8 31.4 all-gather.3
